TPU v7x, 32 devices: a whole 2x2x4 slice. The times are simulated.
32 devices in a mesh: wall: 4 (over y, x), stream: 8 (over z, core).
Axes of the slice: x: 2, y: 2, z: 4, core: 2. Of those that a mesh axis runs over, the one named last changes fastest.
Arguments:
- velocity: float32 [3, 32, 128, 128], P(None, 'wall', 'stream'), may hold values from -6 to 6
- sample_block: int32 [4, 32], P('wall', 'stream'), may hold values from 0 to 127
- sample_member: int32 [4, 32, 1], P('wall', 'stream'), may hold values from 0 to 3; in each aligned block of 4 rows (0 to 3, 4 to 7, ..., all dimensions but the last counted through in order) at most 2 rows name the same one
- k_first: bfloat16 [4, 54, 64], P('wall'), may hold values from -6 to 6
- k_second: bfloat16 [4, 27, 64, 64], P('wall'), may hold values from -6 to 6
- w_hidden: bfloat16 [4, 2048, 2048], P('wall'), may hold values from -6 to 6
- w_out: bfloat16 [4, 2048, 2], P('wall'), may hold values from -6 to 6
Outputs:
- new_field: float32 [3, 32, 128, 128], P(None, 'wall', 'stream')
- stress: float32 [2, 4, 32], P(None, 'wall', 'stream')
- new_k_first: float32 [4, 54, 64], P('wall')
- new_k_second: float32 [4, 27, 64, 64], P('wall')
- new_w_hidden: float32 [4, 2048, 2048], P('wall', 'stream')
- new_w_out: float32 [4, 2048, 2], P('wall')
Inputs may be any that keep to these rules, and one draw needn't show every extreme that they name: `sample_member`: in the list of one slab at most 2 samples name the same member; in every draw some slab names some member exactly 2 times.
All inputs are finite; a program needn't handle non-finite values.
Results may differ from a plain program's by a relative error of at most 0.0064.
Values may be sent and summed in bfloat16 or wider, within the bound.
A program may use at most 128 MiB of HBM per device.

v0:
```python
import math

import jax
import jax.numpy as jnp
import numpy as np
from jax import lax
from jax.sharding import PartitionSpec as P

P_SIZE = 8
PY = 4
PX = 4
PZ = 8
CAP = 2
FEATS = 2048


highest = lax.Precision.HIGHEST
time_step = 0.005
relax_rate = 20.0
viscosity = 0.3
learn_rate = 0.5
rms_eps = 1e-06
tap_offsets = [
    (first_off, second_off, third_off)
    for first_off in (-1, 0, 1)
    for second_off in (-1, 0, 1)
    for third_off in (-1, 0, 1)
]


def with_halo(shard, sides, width):
    for axis, dim in sides:
        size, length = (lax.axis_size(axis), shard.shape[dim])
        up = [(i, (i + 1) % size) for i in range(size)]
        down = [(j, i) for i, j in up]
        last = lax.slice_in_dim(shard, length - width, length, axis=dim)
        first = lax.slice_in_dim(shard, 0, width, axis=dim)
        before = lax.ppermute(last, axis, up)
        after = lax.ppermute(first, axis, down)
        shard = jnp.concatenate([before, shard, after], axis=dim)
    return shard


def cheb_tables(points):
    order = points - 1
    node_index = np.arange(points)
    nodes = -np.cos(np.pi * node_index / order)
    end_weight = np.where((node_index == 0) | (node_index == order), 2.0, 1.0)
    parity = (-1.0) ** (node_index[:, None] + node_index[None, :])
    offdiag = 1.0 - np.eye(points)
    spread = nodes[:, None] - nodes[None, :] + np.eye(points)
    deriv = end_weight[:, None] / end_weight[None, :] * parity / spread * offdiag
    deriv = deriv - np.eye(points) * deriv.sum(axis=1)[:, None]
    highpass = parity / (order * end_weight[None, :])
    return (deriv, highpass, 0.5 * order * order)


def axis_matrices(count, periodic):
    deriv, highpass, lift_half = cheb_tables(P_SIZE)
    length = count * P_SIZE
    slope = np.kron(np.eye(count), deriv)
    upper = np.kron(np.eye(count), highpass)
    faces = count if periodic else count - 1
    for element in range(faces):
        last_node = element * P_SIZE + P_SIZE - 1
        next_node = (element + 1) % count * P_SIZE
        slope[last_node, next_node] += lift_half
        slope[last_node, last_node] -= lift_half
        slope[next_node, last_node] -= lift_half
        slope[next_node, next_node] += lift_half
    if not periodic:
        slope[0, 0] += lift_half
        slope[length - 1, length - 1] -= lift_half
    paired = jnp.asarray(np.concatenate([slope, upper], axis=0), jnp.float32)
    return (paired, lift_half)


def slot_matrix(members, member_count):
    member_hot = (members[..., None] == jnp.arange(member_count, dtype=jnp.int32)).astype(jnp.int32)
    before = jnp.cumsum(member_hot, axis=-2) - member_hot
    ranks = jnp.sum(before * member_hot, axis=-1)
    slots = members * CAP + ranks
    return (slots[..., None, :] == jnp.arange(member_count * CAP, dtype=jnp.int32)[:, None]).astype(
        jnp.float32
    )


def shifted(grid, offset):
    padded = jnp.pad(grid, ((0, 0), (1, 1), (1, 1), (1, 1), (0, 0)))
    size_y, size_x, size_z = (grid.shape[1], grid.shape[2], grid.shape[3])
    return padded[
        :,
        1 + offset[0] : 1 + offset[0] + size_y,
        1 + offset[1] : 1 + offset[1] + size_x,
        1 + offset[2] : 1 + offset[2] + size_z,
        :,
    ]


def silu_slope(value):
    gate = jax.nn.sigmoid(value)
    return gate * (1.0 + value * (1.0 - gate))


def forward_back(patches, aim_rows, valid, k_first, k_second, w_hidden, w_out):
    batch = patches.shape[0]
    channels = k_second.shape[-1]
    inputs = patches.reshape(batch, 2, PY, PX, PZ).transpose(0, 2, 3, 4, 1)
    columns = jnp.concatenate([shifted(inputs, offset) for offset in tap_offsets], axis=-1).reshape(
        -1, 54
    )
    scale_one = 1.0 / math.sqrt(54.0)
    scale_two = 1.0 / math.sqrt(27.0 * channels)
    scale_three = 1.0 / math.sqrt(1.0 * w_hidden.shape[0])
    scale_four = 1.0 / math.sqrt(1.0 * w_hidden.shape[1])
    pre_one = jnp.dot(columns, k_first, preferred_element_type=jnp.float32) * scale_one
    hidden_one = jax.nn.silu(pre_one).astype(jnp.bfloat16).reshape(batch, PY, PX, PZ, channels)
    pre_two = jnp.zeros((batch * PY * PX * PZ, channels), jnp.float32)
    for tap_index in range(27):
        moved = shifted(hidden_one, tap_offsets[tap_index]).reshape(-1, channels)
        pre_two = pre_two + jnp.dot(moved, k_second[tap_index], preferred_element_type=jnp.float32)
    pre_two = pre_two * scale_two
    pooled = (
        jax.nn.silu(pre_two).reshape(batch, PY // 2, 2, PX // 2, 2, PZ, channels).mean(axis=(2, 4))
    )
    features = pooled.reshape(batch, -1).astype(jnp.bfloat16)
    pre_three = jnp.dot(features, w_hidden, preferred_element_type=jnp.float32) * scale_three
    hidden_three = jax.nn.silu(pre_three).astype(jnp.bfloat16)
    pred = jnp.dot(hidden_three, w_out, preferred_element_type=jnp.float32) * scale_four
    error = valid.astype(jnp.float32)[:, None] * (pred - aim_rows.astype(jnp.float32))
    grad_out = jnp.dot(hidden_three.astype(jnp.float32).T, error, precision=highest) * scale_four
    delta_three = (
        jnp.dot(error, w_out.astype(jnp.float32).T, precision=highest)
        * scale_four
        * silu_slope(pre_three)
    ).astype(jnp.bfloat16)
    back_feat = jnp.dot(delta_three, w_hidden.T, preferred_element_type=jnp.float32) * scale_three
    back_grid = back_feat.reshape(batch, PY // 2, 1, PX // 2, 1, PZ, channels)
    spread_back = (
        jnp.broadcast_to(back_grid, (batch, PY // 2, 2, PX // 2, 2, PZ, channels)).reshape(
            -1, channels
        )
        * 0.25
    )
    delta_two = (spread_back * silu_slope(pre_two)).astype(jnp.bfloat16)
    delta_grid = delta_two.reshape(batch, PY, PX, PZ, channels)
    grad_two = []
    back_one = jnp.zeros((batch * PY * PX * PZ, channels), jnp.float32)
    for tap_index in range(27):
        offset = tap_offsets[tap_index]
        moved = shifted(hidden_one, offset).reshape(-1, channels)
        grad_two.append(jnp.dot(moved.T, delta_two, preferred_element_type=jnp.float32) * scale_two)
        mirror = (-offset[0], -offset[1], -offset[2])
        back_one = back_one + jnp.dot(
            shifted(delta_grid, mirror).reshape(-1, channels),
            k_second[tap_index].T,
            preferred_element_type=jnp.float32,
        )
    delta_one = (back_one * scale_two * silu_slope(pre_one)).astype(jnp.bfloat16)
    grad_one = jnp.dot(columns.T, delta_one, preferred_element_type=jnp.float32) * scale_one
    return (pred, grad_one, jnp.stack(grad_two), grad_out, features, delta_three)


def row_update(weight, grad):
    scale = jnp.sqrt(jnp.mean(grad * grad, axis=-1, keepdims=True) + rms_eps)
    return weight.astype(jnp.float32) - learn_rate * grad / scale


def whole_update(weight, grad):
    scale = jnp.sqrt(jnp.mean(grad * grad) + rms_eps)
    return weight.astype(jnp.float32) - learn_rate * grad / scale


def body(velocity, sample_block, sample_member, k_first, k_second, w_hidden, w_out):
    wall_count = lax.axis_size("wall")
    wall_place = lax.axis_index("wall")
    flow_count = lax.axis_size("stream")
    flow_place = lax.axis_index("stream")
    padded = with_halo(velocity, (("wall", 1), ("stream", 2)), 1)
    keep_low = (wall_place > 0).astype(jnp.float32)
    keep_high = (wall_place < wall_count - 1).astype(jnp.float32)
    below = padded[:, 0, 1:-1, :] * keep_low
    above = padded[:, -1, 1:-1, :] * keep_high
    left_face = padded[:, 1:-1, 0, :]
    right_face = padded[:, 1:-1, -1, :]
    size_y, size_x, size_z = (velocity.shape[1], velocity.shape[2], velocity.shape[3])
    pair_y, lift_half = axis_matrices(size_y // P_SIZE, False)
    pair_x, lift_same = axis_matrices(size_x // P_SIZE, False)
    pair_z, lift_again = axis_matrices(size_z // P_SIZE, True)
    along_y = jnp.einsum("cyxz,wy->cwxz", velocity, pair_y, precision=highest)
    grad_y = (
        along_y[:, :size_y]
        .at[:, 0]
        .add(-lift_half * below)
        .at[:, size_y - 1]
        .add(lift_half * above)
    )
    high_y = along_y[:, size_y:]
    along_x = jnp.einsum("cyxz,wx->cywz", velocity, pair_x, precision=highest)
    grad_x = (
        along_x[:, :, :size_x]
        .at[:, :, 0]
        .add(-lift_half * left_face)
        .at[:, :, size_x - 1]
        .add(lift_half * right_face)
    )
    high_x = along_x[:, :, size_x:]
    along_z = jnp.einsum("cyxz,wz->cyxw", velocity, pair_z, precision=highest)
    grad_z = along_z[..., :size_z]
    high_z = along_z[..., size_z:]
    advect = velocity[0][None] * grad_x + velocity[1][None] * grad_y + velocity[2][None] * grad_z
    new_field = velocity + time_step * (-advect - relax_rate * (high_x + high_y + high_z))
    rows_y, rows_x, rows_z = (size_y // PY, size_x // PX, size_z // PZ)
    tangent = jnp.stack([velocity[0], velocity[2]]).reshape(2, rows_y, PY, rows_x, PX, rows_z, PZ)
    blocks = tangent.transpose(1, 3, 5, 0, 2, 4, 6).reshape(-1, 2 * PY * PX * PZ)
    slope_wall = jnp.stack([grad_y[0], grad_y[2]]).reshape(2, rows_y, PY, rows_x, PX, rows_z, PZ)
    stress_true = (
        (viscosity * jnp.mean(slope_wall, axis=(2, 4, 6))).transpose(1, 2, 3, 0).reshape(-1, 2)
    )
    picked = sample_block.reshape(-1)
    members = sample_member.reshape(-1)
    patch_rows = jnp.take(blocks, picked, axis=0).astype(jnp.bfloat16)
    aim_rows = jnp.take(stress_true, picked, axis=0).astype(jnp.bfloat16)
    select = slot_matrix(members, wall_count)
    select_half = select.astype(jnp.bfloat16)
    send_rows = jnp.dot(select_half, patch_rows, preferred_element_type=jnp.float32).astype(
        jnp.bfloat16
    )
    send_aims = jnp.dot(select_half, aim_rows, preferred_element_type=jnp.float32).astype(
        jnp.bfloat16
    )
    send_valid = jnp.sum(select, axis=1).astype(jnp.bfloat16)
    recv_rows, recv_aims, recv_valid = (
        lax.all_to_all(send_rows, "wall", split_axis=0, concat_axis=0, tiled=True),
        lax.all_to_all(send_aims, "wall", split_axis=0, concat_axis=0, tiled=True),
        lax.all_to_all(send_valid, "wall", split_axis=0, concat_axis=0, tiled=True),
    )
    pred, grad_one, grad_two, grad_out, features, delta_three = forward_back(
        recv_rows, recv_aims, recv_valid, k_first[0], k_second[0], w_hidden[0], w_out[0]
    )
    back = lax.all_to_all(pred, "wall", split_axis=0, concat_axis=0, tiled=True)
    stress_local = jnp.dot(select.T, back, precision=highest)
    stress = stress_local.T[:, None, :]
    share_rows = FEATS // flow_count
    dense_scale = 1.0 / math.sqrt(1.0 * FEATS)
    columns_here = lax.all_to_all(features, "stream", split_axis=1, concat_axis=0, tiled=True)
    grad_hidden = (
        jnp.dot(
            columns_here.T,
            lax.all_gather(delta_three, "stream", axis=0, tiled=True),
            preferred_element_type=jnp.float32,
        )
        * dense_scale
    )
    own_rows = lax.dynamic_slice_in_dim(w_hidden[0], flow_place * share_rows, share_rows, 0)
    new_w_hidden = row_update(own_rows, grad_hidden)[None]
    grad_one, grad_two, grad_out = lax.psum((grad_one, grad_two, grad_out), "stream")
    new_k_second = row_update(k_second[0], grad_two)
    new_k_first = row_update(k_first[0], grad_one)
    new_w_out = whole_update(w_out[0], grad_out)
    return (new_field, stress, new_k_first[None], new_k_second[None], new_w_hidden, new_w_out[None])


def solution(mesh):
    placed = (
        P(None, "wall", "stream", None),
        P("wall", "stream"),
        P("wall", "stream", None),
        P("wall", None, None),
        P("wall", None, None, None),
        P("wall", None, None),
        P("wall", None, None),
    )
    return jax.shard_map(
        body,
        mesh=mesh,
        in_specs=placed,
        out_specs=(
            P(None, "wall", "stream", None),
            P(None, "wall", "stream"),
            P("wall", None, None),
            P("wall", None, None, None),
            P("wall", "stream", None),
            P("wall", None, None),
        ),
        check_vma=False,
    )
```

profile of v0, /device:TPU:0, one launch (start us, length us, event | category | flops | bytes accessed | tf_op | source)
XLA Modules:
  0.0 252.3 jit_solution(3895413117062613057)
XLA Ops:
  10.2 5.2 %all-to-all-start.2 = ((bf16[4,2,1]{1,2,0:T(2,128)(2,1)}), bf16[4,2,1]{1,2,0:T(2,128)(2,1)S(1)}, u32[]{:S(2)}, u32[]{:S(2)}) async-start(bf16[4,2,1]{1,2,0:T(2,128)(2,1)} %convert_element_type.250), calls=%async_computation.2 | async-start | bytes 4096 | tf_op jit(solution)/shard_map/all_to_all | solution.py:236
  16.8 2.9 %collective-permute-start.1 = (f32[3,1,16,128]{3,2,1,0:T(8,128)}, f32[3,1,16,128]{3,2,1,0:T(8,128)}, u32[]{:S(2)}, u32[]{:S(2)}) collective-permute-start(f32[3,1,16,128]{3,2,1,0:T(8,128)} %get-tuple-element.153), channel_id=1, source_target_pairs={{8,0},{16,8},{24,16},{0,24},{9,1},{17,9},{25,17},{1,25},{10,2},{18... | collective-permute-start | bytes 73736 | tf_op jit(solution)/shard_map/ppermute | solution.py:39
  21.9 1.6 slice_bitcast_fusion.2
  32.1 4.2 %all-to-all-start = ((bf16[4,2,256]{2,1,0:T(2,128)(2,1)}), bf16[4,2,256]{2,1,0:T(2,128)(2,1)S(1)}, u32[]{:S(2)}, u32[]{:S(2)}) async-start(bf16[4,2,256]{2,1,0:T(2,128)(2,1)} %all_to_all.36), calls=%async_computation | async-start | bytes 8192 | tf_op jit(solution)/shard_map/all_to_all | solution.py:234
  36.9 4.1 %all-to-all-done = bf16[4,2,256]{2,1,0:T(2,128)(2,1)S(1)} async-done(((bf16[4,2,256]{2,1,0:T(2,128)(2,1)}), bf16[4,2,256]{2,1,0:T(2,128)(2,1)S(1)}, u32[]{:S(2)}, u32[]{:S(2)}) %all-to-all-start) | async-done | bytes 4128 | tf_op jit(solution)/shard_map/all_to_all | solution.py:234
  52.1 1.7 copy.139
  53.8 2.4 copy.140
  56.1 2.4 copy.141
  58.5 2.4 copy.142
  60.9 2.4 copy.143
  63.2 2.4 copy.144
  67.2 2.4 copy.146
  69.6 2.4 copy.147
  71.9 2.4 copy.148
  74.3 2.4 copy.150
  76.7 2.4 copy.151
  79.0 2.4 copy.152
  81.4 2.4 copy.153
  85.3 1.5 copy.155
  86.8 6.4 %concatenate.15 = bf16[8,4,4,8,54]{4,3,2,1,0:T(8,128)(2,1)} concatenate(bf16[8,4,4,8,2]{4,3,2,1,0:T(8,128)(2,1)S(1)} %copy.136, bf16[8,4,4,8,2]{4,3,2,1,0:T(8,128)(2,1)S(1)} %copy.137, bf16[8,4,4,8,2]{4,3,2,1,0:T(8,128)(2,1)S(1)} %copy.138, bf16[8,4,4,8,2]{4,3,2,1,0:T(8,128)(2,1)S(1)} %copy.139, bf16[8,4,4,8,2]{4,3,2,1,0:T(8,128)(2,1)} %copy.140, ...), dimensions={4} | concatenate | bytes 221184 | tf_op jit(solution)/shard_map/concatenate | solution.py:109
  93.2 1.9 multiply_convert_fusion.1
  106.7 5.2 %multiply_convert_fusion.3 = (bf16[8,2048]{1,0:T(8,128)(2,1)S(1)}, f32[8,2048]{1,0:T(8,128)}) fusion(bf16[8,2048]{1,0:T(8,128)(2,1)S(1)} %convert_element_type.226, bf16[1,2048,2048]{2,1,0:T(8,128)(2,1)} %param.23), kind=kOutput, calls=%fused_computation.267 | convolution fusion | flops 67207168 | bytes 8519680 | tf_op jit(solution)/shard_map/dot_general | solution.py:127
  112.8 7.0 %all_to_all.52 = f32[4,2,2]{1,2,0:T(2,128)S(1)} all-to-all(f32[4,2,2]{1,2,0:T(2,128)S(1)} %copy.165), channel_id=1, replica_groups=mesh['wall'=4,'stream'=8] {'wall'}, dimensions={0} | all-to-all | bytes 128 | tf_op jit(solution)/shard_map/all_to_all | solution.py:241
  124.0 2.1 reshape.580
  129.5 7.0 %all_to_all.53 = bf16[4,2,2]{1,2,0:T(2,128)(2,1)S(1)} all-to-all(bf16[4,2,2]{1,2,0:T(2,128)(2,1)S(1)} %copy.169), channel_id=1, replica_groups=mesh['wall'=4,'stream'=8] {'wall'}, dimensions={0} | all-to-all | bytes 64 | tf_op jit(solution)/shard_map/all_to_all | solution.py:235
  136.5 4.9 %all-to-all-start.4 = ((bf16[8,8,256]{2,0,1:T(8,128)(2,1)}), bf16[8,8,256]{2,0,1:T(8,128)(2,1)}, u32[]{:S(2)}, u32[]{:S(2)}) async-start(bf16[8,8,256]{2,0,1:T(8,128)(2,1)} %copy.174), calls=%async_computation.4 | async-start | bytes 65536 | tf_op jit(solution)/shard_map/all_to_all | solution.py:246
  144.5 5.6 %fusion.8 = f32[8,2048]{1,0:T(8,128)S(1)} fusion(bf16[8,2048]{1,0:T(8,128)(2,1)S(1)} %fusion.11, bf16[1,2048,2048]{2,1,0:T(8,128)(2,1)} %param.23), kind=kOutput, calls=%fused_computation.61 | convolution fusion | flops 67125248 | bytes 8486912 | tf_op jit(solution)/shard_map/dot_general | solution.py:137
  153.7 2.7 %pad_slice_fusion = (bf16[8,4,4,8,64]{4,3,2,1,0:T(8,128)(2,1)}, bf16[8,4,4,8,64]{4,3,2,1,0:T(8,128)(2,1)}, bf16[8,4,4,8,64]{4,3,2,1,0:T(8,128)(2,1)}, bf16[8,4,4...) fusion(bf16[8,4,4,8,64]{4,3,2,1,0:T(8,128)(2,1)S(1)} %bitcast.562), kind=kLoop, calls=%fused_computation.2 | loop fusion | bytes 2621440 | tf_op jit(solution)/shard_map/slice | solution.py:91
  188.8 29.8 %all-reduce.3 = (f32[54,64]{1,0:T(8,128)S(1)}, f32[2048,2]{0,1:T(2,128)S(1)}) all-reduce(f32[54,64]{1,0:T(8,128)S(1)} %fusion.74, f32[2048,2]{0,1:T(2,128)S(1)} %copy-done.94), channel_id=1, replica_groups=mesh['wall'=4,'stream'=8] {'stream'}, use_global_device_ids=true, to_apply=%region_5.6 | all-reduce | flops 7552 | bytes 60416 | tf_op jit(solution)/shard_map/psum | solution.py:257
  220.8 14.4 %all_gather.3 = bf16[64,2048]{1,0:T(8,128)(2,1)S(1)} all-gather(bf16[8,2048]{1,0:T(8,128)(2,1)S(1)} %fusion.11), channel_id=1, replica_groups=mesh['wall'=4,'stream'=8] {'stream'}, dimensions={0}, use_global_device_ids=true | all-gather | bytes 294912 | tf_op jit(solution)/shard_map/all_gather | solution.py:250
  239.6 3.0 %fusion.12 = f32[1,256,2048]{2,1,0:T(8,128)} fusion(f32[256,2048]{1,0:T(8,128)S(1)} %get-tuple-element.192, f32[256]{0:T(256)S(1)} %add_sqrt_fusion.1, bf16[1,2048,2048]{2,1,0:T(8,128)(2,1)} %param.23, s32[]{:T(128)S(6)} %select_n.33), kind=kLoop, calls=%fused_computation.65 | loop fusion | flops 2097152 | bytes 5243908 | tf_op jit(solution)/shard_map/broadcast_in_dim | solution.py:256
  242.7 1.5 multiply_reduce_fusion.1
  (401 shorter events, 94.8 us)
Async XLA Ops:
  7.2 18.6 %copy-start.100 = (f32[16,8,1,1]{0,1,3,2:T(8,128)S(1)}, f32[16,8,1,1]{0,1,3,2:T(8,128)}, u32[]{:S(2)}) copy-start(f32[16,8,1,1]{0,1,3,2:T(8,128)} %constant.246) | copy-start | bytes 1540
  7.2 18.6 %copy-start = (f32[3,8,16,128]{3,2,1,0:T(8,128)S(1)}, f32[3,8,16,128]{3,2,1,0:T(8,128)}, u32[]{:S(2)}) copy-start(f32[3,8,16,128]{3,2,1,0:T(8,128)} %param.18) | copy-start | bytes 589828
  9.5 21.8 %copy-start.102 = (s32[4]{0:T(128)}, s32[4]{0:T(128)S(1)}, u32[]{:S(2)}) copy-start(s32[4]{0:T(128)S(1)} %multiply_add_fusion) | copy-start | bytes 52
  10.2 21.9 %all-to-all-start.2 = ((bf16[4,2,1]{1,2,0:T(2,128)(2,1)}), bf16[4,2,1]{1,2,0:T(2,128)(2,1)S(1)}, u32[]{:S(2)}, u32[]{:S(2)}) async-start(bf16[4,2,1]{1,2,0:T(2,128)(2,1)} %convert_element_type.250), calls=%async_computation.2 | async-start | bytes 4096 | tf_op jit(solution)/shard_map/all_to_all | solution.py:236
  16.8 104.6 %collective-permute-start.1 = (f32[3,1,16,128]{3,2,1,0:T(8,128)}, f32[3,1,16,128]{3,2,1,0:T(8,128)}, u32[]{:S(2)}, u32[]{:S(2)}) collective-permute-start(f32[3,1,16,128]{3,2,1,0:T(8,128)} %get-tuple-element.153), channel_id=1, source_target_pairs={{8,0},{16,8},{24,16},{0,24},{9,1},{17,9},{25,17},{1,25},{10,2},{18... | collective-permute-start | bytes 73736 | tf_op jit(solution)/shard_map/ppermute | solution.py:39
  19.7 100.9 %collective-permute-start = (f32[3,1,16,128]{3,2,1,0:T(8,128)}, f32[3,1,16,128]{3,2,1,0:T(8,128)}, u32[]{:S(2)}, u32[]{:S(2)}) collective-permute-start(f32[3,1,16,128]{3,2,1,0:T(8,128)} %get-tuple-element.154), channel_id=1, source_target_pairs={{0,8},{8,16},{16,24},{24,0},{1,9},{9,17},{17,25},{25,1},{2,10},{10... | collective-permute-start | bytes 73736 | tf_op jit(solution)/shard_map/ppermute | solution.py:38
  20.4 10.9 %copy-start.104 = (pred[4]{0:T(512)(128)(4,1)}, pred[4]{0:T(512)(128)(4,1)S(1)}, u32[]{:S(2)}) copy-start(pred[4]{0:T(512)(128)(4,1)S(1)} %compare_and_fusion) | copy-start | bytes 16
  23.5 7.1 %copy-start.99 = (s32[1024]{0:T(1024)}, s32[1024]{0:T(1024)S(1)}, u32[]{:S(2)}) copy-start(s32[1024]{0:T(1024)S(1)} %pad_clamp_fusion) | copy-start | bytes 12292
  32.1 8.9 %all-to-all-start = ((bf16[4,2,256]{2,1,0:T(2,128)(2,1)}), bf16[4,2,256]{2,1,0:T(2,128)(2,1)S(1)}, u32[]{:S(2)}, u32[]{:S(2)}) async-start(bf16[4,2,256]{2,1,0:T(2,128)(2,1)} %all_to_all.36), calls=%async_computation | async-start | bytes 8192 | tf_op jit(solution)/shard_map/all_to_all | solution.py:234
  51.2 14.4 %copy-start.91 = (bf16[8,4,4,8,2]{3,2,1,4,0:T(4,128)(2,1)S(1)}, bf16[8,4,4,8,2]{3,2,1,4,0:T(4,128)(2,1)}, u32[]{:S(2)}) copy-start(bf16[8,4,4,8,2]{3,2,1,4,0:T(4,128)(2,1)} %get-tuple-element.164) | copy-start | bytes 12292
  67.1 16.6 %copy-start.90 = (bf16[8,4,4,8,2]{3,2,1,4,0:T(4,128)(2,1)S(1)}, bf16[8,4,4,8,2]{3,2,1,4,0:T(4,128)(2,1)}, u32[]{:S(2)}) copy-start(bf16[8,4,4,8,2]{3,2,1,4,0:T(4,128)(2,1)} %get-tuple-element.172) | copy-start | bytes 12292
  96.3 7.0 %copy-start.41 = (bf16[8,4,4,8,64]{4,3,2,1,0:T(8,128)(2,1)}, bf16[8,4,4,8,64]{4,3,2,1,0:T(8,128)(2,1)S(1)}, u32[]{:S(2)}) copy-start(bf16[8,4,4,8,64]{4,3,2,1,0:T(8,128)(2,1)S(1)} %get-tuple-element.139) | copy-start | bytes 393220
  96.3 7.2 %copy-start.39 = (bf16[8,4,4,8,64]{4,3,2,1,0:T(8,128)(2,1)}, bf16[8,4,4,8,64]{4,3,2,1,0:T(8,128)(2,1)S(1)}, u32[]{:S(2)}) copy-start(bf16[8,4,4,8,64]{4,3,2,1,0:T(8,128)(2,1)S(1)} %get-tuple-element.140) | copy-start | bytes 393220
  96.3 7.5 %copy-start.37 = (bf16[8,4,4,8,64]{4,3,2,1,0:T(8,128)(2,1)}, bf16[8,4,4,8,64]{4,3,2,1,0:T(8,128)(2,1)S(1)}, u32[]{:S(2)}) copy-start(bf16[8,4,4,8,64]{4,3,2,1,0:T(8,128)(2,1)S(1)} %get-tuple-element.141) | copy-start | bytes 393220
  96.4 7.7 %copy-start.35 = (bf16[8,4,4,8,64]{4,3,2,1,0:T(8,128)(2,1)}, bf16[8,4,4,8,64]{4,3,2,1,0:T(8,128)(2,1)S(1)}, u32[]{:S(2)}) copy-start(bf16[8,4,4,8,64]{4,3,2,1,0:T(8,128)(2,1)S(1)} %get-tuple-element.142) | copy-start | bytes 393220
  96.4 8.0 %copy-start.33 = (bf16[8,4,4,8,64]{4,3,2,1,0:T(8,128)(2,1)}, bf16[8,4,4,8,64]{4,3,2,1,0:T(8,128)(2,1)S(1)}, u32[]{:S(2)}) copy-start(bf16[8,4,4,8,64]{4,3,2,1,0:T(8,128)(2,1)S(1)} %get-tuple-element.137) | copy-start | bytes 393220
  106.7 13.2 %copy-start.103 = (s32[4]{0:T(128)S(1)}, s32[4]{0:T(128)}, u32[]{:S(2)}) copy-start(s32[4]{0:T(128)} %copy-done.102) | copy-start | bytes 52
  106.7 13.9 %copy-start.52 = (f32[3,8,16,128]{3,2,1,0:T(8,128)S(1)}, f32[3,8,16,128]{3,2,1,0:T(8,128)}, u32[]{:S(2)}) copy-start(f32[3,8,16,128]{3,2,1,0:T(8,128)} %slice.699) | copy-start | bytes 589828
  122.8 113.8 %collective-permute-start.3 = (f32[3,10,1,128]{3,2,1,0:T(1,128)}, f32[3,10,1,128]{3,2,1,0:T(1,128)}, u32[]{:S(2)}, u32[]{:S(2)}) collective-permute-start(f32[3,10,1,128]{3,2,1,0:T(1,128)} %get-tuple-element.144), channel_id=1, source_target_pairs={{1,0},{2,1},{3,2},{4,3},{5,4},{6,5},{7,6},{0,7},{9,8},{10,9},{11,1... | collective-permute-start | bytes 46088 | tf_op jit(solution)/shard_map/ppermute | solution.py:39
  122.8 113.0 %collective-permute-start.2 = (f32[3,10,1,128]{3,2,1,0:T(1,128)}, f32[3,10,1,128]{3,2,1,0:T(1,128)}, u32[]{:S(2)}, u32[]{:S(2)}) collective-permute-start(f32[3,10,1,128]{3,2,1,0:T(1,128)} %get-tuple-element.145), channel_id=1, source_target_pairs={{0,1},{1,2},{2,3},{3,4},{4,5},{5,6},{6,7},{7,0},{8,9},{9,10},{10,1... | collective-permute-start | bytes 46088 | tf_op jit(solution)/shard_map/ppermute | solution.py:38
  136.5 101.8 %all-to-all-start.4 = ((bf16[8,8,256]{2,0,1:T(8,128)(2,1)}), bf16[8,8,256]{2,0,1:T(8,128)(2,1)}, u32[]{:S(2)}, u32[]{:S(2)}) async-start(bf16[8,8,256]{2,0,1:T(8,128)(2,1)} %copy.174), calls=%async_computation.4 | async-start | bytes 65536 | tf_op jit(solution)/shard_map/all_to_all | solution.py:246
  141.4 101.3 %all-reduce.6.cloned.1.call-start = ((), (), s32[]{:S(2)}) async-start(), calls=%async_computation.5 | async-start | bytes 1769472 | tf_op jit(solution)/shard_map/psum | solution.py:257
  187.1 32.9 %copy-start.96 = (bf16[1,54,64]{2,1,0:T(8,128)(2,1)S(1)}, bf16[1,54,64]{2,1,0:T(8,128)(2,1)}, u32[]{:S(2)}) copy-start(bf16[1,54,64]{2,1,0:T(8,128)(2,1)} %param.21) | copy-start | bytes 20740
  187.2 33.0 %copy-start.98 = (bf16[1,2048,2]{1,2,0:T(2,128)(2,1)S(1)}, bf16[1,2048,2]{1,2,0:T(2,128)(2,1)}, u32[]{:S(2)}) copy-start(bf16[1,2048,2]{1,2,0:T(2,128)(2,1)} %param.24) | copy-start | bytes 24580
  187.3 48.6 %copy-start.50 = (f32[3,8,32,128]{3,2,1,0:T(8,128)S(1)}, f32[3,8,32,128]{3,2,1,0:T(8,128)}, u32[]{:S(2)}) copy-start(f32[3,8,32,128]{3,2,1,0:T(8,128)} %copy-done.49) | copy-start | bytes 1179652
  187.3 49.3 %slice-start = ((f32[3,8,32,128]{3,2,1,0:T(8,128)}), f32[3,8,16,128]{3,2,1,0:T(8,128)S(1)}, s32[]{:S(2)}) async-start(f32[3,8,32,128]{3,2,1,0:T(8,128)} %copy-done.49), calls=%async_computation.6 | async-start | bytes 393216 | tf_op jit(solution)/shard_map/slice | solution.py:201
  187.3 50.2 %copy-start.48 = (f32[16,3,16,128]{3,2,0,1:T(8,128)S(1)}, f32[16,3,16,128]{3,2,0,1:T(8,128)}, u32[]{:S(2)}) copy-start(f32[16,3,16,128]{3,2,0,1:T(8,128)} %copy-done.47) | copy-start | bytes 1179652
  187.3 50.2 %copy-start.51 = (f32[3,8,16,256]{3,2,1,0:T(8,128)S(1)}, f32[3,8,16,256]{3,2,1,0:T(8,128)}, u32[]{:S(2)}) copy-start(f32[3,8,16,256]{3,2,1,0:T(8,128)} %convolution_bitcast_fusion) | copy-start | bytes 1179652
  187.3 50.2 %copy-start.54 = (f32[3,8,16,128]{3,2,1,0:T(8,128)S(1)}, f32[3,8,16,128]{3,2,1,0:T(8,128)}, u32[]{:S(2)}) copy-start(f32[3,8,16,128]{3,2,1,0:T(8,128)} %copy-done.53) | copy-start | bytes 589828
  187.3 50.2 %copy-start.85 = (f32[8,16,128]{2,1,0:T(8,128)S(1)}, f32[8,16,128]{2,1,0:T(8,128)}, u32[]{:S(2)}) copy-start(f32[8,16,128]{2,1,0:T(8,128)} %get-tuple-element.150) | copy-start | bytes 196612
  187.3 50.2 %copy-start.86 = (f32[8,16,128]{2,1,0:T(8,128)S(1)}, f32[8,16,128]{2,1,0:T(8,128)}, u32[]{:S(2)}) copy-start(f32[8,16,128]{2,1,0:T(8,128)} %get-tuple-element.151) | copy-start | bytes 196612
  187.3 50.2 %copy-start.87 = (f32[8,16,128]{2,1,0:T(8,128)S(1)}, f32[8,16,128]{2,1,0:T(8,128)}, u32[]{:S(2)}) copy-start(f32[8,16,128]{2,1,0:T(8,128)} %get-tuple-element.152) | copy-start | bytes 196612
  (82 other events, 222.2 us)
Sparse Core Ops, SparseCore 0:
  178.8 56.7 all-reduce.5
where the time goes:
time: 255 us; the launch traced here: 252 us
  local copies, waits for them, and re-layouts  79.9 us (31%)
  matrix products  58.8 us (23%)
  blocking collectives  58.2 us (23%)
  starting transfers between devices  18 us (7%)
  other arithmetic  17.1 us (7%)
  between operations  16.2 us (6%)
  waiting for transfers between devices  4.09 us (2%)
    slice x32, local copies, waits for them, and re-layouts, shifted(): padded[:, 1 + offset[0]:1 + offset[0] + size_y, 1 + offset[1]:1 + offset[...  50.6 us
    psum x1, blocking collectives, body(): lax.psum((grad_one, grad_two, grad_out), 'stream')  29.8 us
    dot_general x27, matrix products, forward_back(): jnp.dot(moved.T, delta_two, preferred_element_type=jnp.float32) * scale_two  22.9 us
    all_gather x1, blocking collectives, body(): lax.all_gather(delta_three, 'stream', axis=0, tiled=True)  14.4 us
    dot_general x27, matrix products, forward_back(): jnp.dot(moved, k_second[tap_index], preferred_element_type=jnp.float32)  7.2 us
    all_to_all x1, blocking collectives, body(): back = lax.all_to_all(pred, 'wall', split_axis=0, concat_axis=0, tiled=True)  7 us
    all_to_all x1, blocking collectives, body(): lax.all_to_all(send_aims, 'wall', split_axis=0, concat_axis=0, tiled=True)  6.98 us
    unnamed x212, local copies, waits for them, and re-layouts  6.51 us
  transfers between devices with their start and end apart: 8, of which 1 were waited for; matrix products, arithmetic and copies ran while one was open for 56% of the time, Pallas kernels for 0%

commit v1 on v0

--- a/solution.py
+++ b/solution.py
@@ -4,6 +4,8 @@
 import jax.numpy as jnp
 import numpy as np
 from jax import lax
+from jax.experimental import pallas as pl
+from jax.experimental.pallas import tpu as pltpu
 from jax.sharding import PartitionSpec as P
 
 P_SIZE = 8
@@ -85,80 +87,169 @@
     )
 
 
-def shifted(grid, offset):
-    padded = jnp.pad(grid, ((0, 0), (1, 1), (1, 1), (1, 1), (0, 0)))
-    size_y, size_x, size_z = (grid.shape[1], grid.shape[2], grid.shape[3])
-    return padded[
-        :,
-        1 + offset[0] : 1 + offset[0] + size_y,
-        1 + offset[1] : 1 + offset[1] + size_x,
-        1 + offset[2] : 1 + offset[2] + size_z,
-        :,
-    ]
+def sigmoid(value):
+    return 1.0 / (1.0 + jnp.exp(-value))
 
 
 def silu_slope(value):
-    gate = jax.nn.sigmoid(value)
+    gate = sigmoid(value)
     return gate * (1.0 + value * (1.0 - gate))
 
 
-def forward_back(patches, aim_rows, valid, k_first, k_second, w_hidden, w_out):
-    batch = patches.shape[0]
-    channels = k_second.shape[-1]
-    inputs = patches.reshape(batch, 2, PY, PX, PZ).transpose(0, 2, 3, 4, 1)
-    columns = jnp.concatenate([shifted(inputs, offset) for offset in tap_offsets], axis=-1).reshape(
-        -1, 54
-    )
+def z_shifts(grid, sign):
+    edge = jnp.zeros((16, 1, grid.shape[2], grid.shape[-1]), grid.dtype)
+    before = jnp.concatenate([edge, grid[:, :-1]], axis=1)
+    after = jnp.concatenate([grid[:, 1:], edge], axis=1)
+    parts = [before, grid, after] if sign > 0 else [after, grid, before]
+    return jnp.concatenate([part.reshape(-1, grid.shape[-1]) for part in parts], axis=-1)
+
+
+def window(padded, first, second):
+    return padded[1 + first : 5 + first, 1 + second : 5 + second].reshape(-1, padded.shape[-1])
+
+
+def clear_border(padded):
+    row = jnp.zeros((1, 6) + padded.shape[2:], padded.dtype)
+    column = jnp.zeros((6, 1) + padded.shape[2:], padded.dtype)
+    padded[0:1] = row
+    padded[5:6] = row
+    padded[:, 0:1] = column
+    padded[:, 5:6] = column
+
+
+def matmul(left, right, dims=((1,), (0,))):
+    return lax.dot_general(left, right, (dims, ((), ())), preferred_element_type=jnp.float32)
+
+
+def network(
+    rows, aims, valid, k_first, k_second, k_back, w_hbm, w_out,
+    pred_ref, grad_one_ref, grad_two_ref, grad_out_ref, feat_ref, delta_ref,
+    w_vmem, cols, pre_one, hid_pad, del_pad, mid_pad, pre_two, pooled, w_sem,
+):
+    batch = rows.shape[0]
+    points = 128 * batch
+    fetch = pltpu.make_async_copy(w_hbm, w_vmem, w_sem)
+    fetch.start()
     scale_one = 1.0 / math.sqrt(54.0)
-    scale_two = 1.0 / math.sqrt(27.0 * channels)
-    scale_three = 1.0 / math.sqrt(1.0 * w_hidden.shape[0])
-    scale_four = 1.0 / math.sqrt(1.0 * w_hidden.shape[1])
-    pre_one = jnp.dot(columns, k_first, preferred_element_type=jnp.float32) * scale_one
-    hidden_one = jax.nn.silu(pre_one).astype(jnp.bfloat16).reshape(batch, PY, PX, PZ, channels)
-    pre_two = jnp.zeros((batch * PY * PX * PZ, channels), jnp.float32)
-    for tap_index in range(27):
-        moved = shifted(hidden_one, tap_offsets[tap_index]).reshape(-1, channels)
-        pre_two = pre_two + jnp.dot(moved, k_second[tap_index], preferred_element_type=jnp.float32)
-    pre_two = pre_two * scale_two
-    pooled = (
-        jax.nn.silu(pre_two).reshape(batch, PY // 2, 2, PX // 2, 2, PZ, channels).mean(axis=(2, 4))
-    )
-    features = pooled.reshape(batch, -1).astype(jnp.bfloat16)
-    pre_three = jnp.dot(features, w_hidden, preferred_element_type=jnp.float32) * scale_three
-    hidden_three = jax.nn.silu(pre_three).astype(jnp.bfloat16)
-    pred = jnp.dot(hidden_three, w_out, preferred_element_type=jnp.float32) * scale_four
-    error = valid.astype(jnp.float32)[:, None] * (pred - aim_rows.astype(jnp.float32))
-    grad_out = jnp.dot(hidden_three.astype(jnp.float32).T, error, precision=highest) * scale_four
-    delta_three = (
-        jnp.dot(error, w_out.astype(jnp.float32).T, precision=highest)
-        * scale_four
-        * silu_slope(pre_three)
+    scale_two = 1.0 / math.sqrt(1728.0)
+    scale_dense = 1.0 / math.sqrt(2048.0)
+    clear_border(hid_pad)
+    clear_border(del_pad)
+    clear_border(mid_pad)
+    lane = lax.broadcasted_iota(jnp.int32, (batch, 128), 1)
+    at = (lane // 32, (lane // 8) % 4, lane % 8)
+    cols[54 * batch : 64 * batch, :] = jnp.zeros((10 * batch, 128), jnp.float32)
+    channel = [rows[:, 0:128].astype(jnp.float32), rows[:, 128:256].astype(jnp.float32)]
+    for tap, offset in enumerate(tap_offsets):
+        inside = None
+        for place, step, size in zip(at, offset, (4, 4, 8)):
+            if step:
+                good = (place + step >= 0) & (place + step < size)
+                inside = good if inside is None else inside & good
+        turn = (-(offset[0] * 32 + offset[1] * 8 + offset[2])) % 128
+        for c in range(2):
+            moved = channel[c] if turn == 0 else pltpu.roll(channel[c], turn, 1)
+            if inside is not None:
+                moved = jnp.where(inside, moved, 0.0)
+            cols[(2 * tap + c) * batch : (2 * tap + c + 1) * batch, :] = moved
+    columns = jnp.concatenate(
+        [cols[pl.ds(slot, 64, stride=batch), :] for slot in range(batch)], axis=1
     ).astype(jnp.bfloat16)
-    back_feat = jnp.dot(delta_three, w_hidden.T, preferred_element_type=jnp.float32) * scale_three
-    back_grid = back_feat.reshape(batch, PY // 2, 1, PX // 2, 1, PZ, channels)
-    spread_back = (
-        jnp.broadcast_to(back_grid, (batch, PY // 2, 2, PX // 2, 2, PZ, channels)).reshape(
-            -1, channels
+    first = matmul(columns, k_first[...], ((0,), (0,))) * scale_one
+    for slot in range(batch):
+        pre_one[pl.ds(slot, 128, stride=batch), :] = first[slot * 128 : slot * 128 + 128]
+    value = pre_one[...]
+    hidden = (value * sigmoid(value)).astype(jnp.bfloat16).astype(jnp.float32)
+    hidden3 = z_shifts(hidden.reshape(16, 8, batch, 64), 1)
+    hidden_t = hidden3.T.astype(jnp.bfloat16)
+    hid_pad[1:5, 1:5] = hidden3.astype(jnp.bfloat16).reshape(4, 4, 8 * batch, 192)
+    total = jnp.zeros((points, 64), jnp.float32)
+    for pair in range(9):
+        total = total + matmul(window(hid_pad, pair // 3 - 1, pair % 3 - 1), k_second[pair])
+    second = total * scale_two
+    pre_two[...] = second
+    act = (second * sigmoid(second)).reshape(2, 2, 2, 2, 8 * batch, 64)
+    pool = (act[:, 0, :, 0] + act[:, 0, :, 1] + act[:, 1, :, 0] + act[:, 1, :, 1]) * 0.25
+    pieces = pool.reshape(32, batch, 64)
+    features = jnp.concatenate([pieces[i] for i in range(32)], axis=1).astype(jnp.bfloat16)
+    feat_ref[...] = features
+    fetch.wait()
+    third = jnp.concatenate(
+        [matmul(features, w_vmem[:, j * 512 : j * 512 + 512]) for j in range(4)], axis=1
+    ) * scale_dense
+    gate = sigmoid(third)
+    hidden_three = (third * gate).astype(jnp.bfloat16).astype(jnp.float32)
+    errors = []
+    for i in range(2):
+        pred = jnp.sum(hidden_three * w_out[i : i + 1, :], axis=1, keepdims=True) * scale_dense
+        pred_ref[:, i : i + 1] = pred
+        error = valid[...] * (pred - aims[:, i : i + 1])
+        grad_out_ref[i : i + 1, :] = (
+            jnp.sum(hidden_three * error, axis=0, keepdims=True) * scale_dense
         )
-        * 0.25
-    )
-    delta_two = (spread_back * silu_slope(pre_two)).astype(jnp.bfloat16)
-    delta_grid = delta_two.reshape(batch, PY, PX, PZ, channels)
-    grad_two = []
-    back_one = jnp.zeros((batch * PY * PX * PZ, channels), jnp.float32)
-    for tap_index in range(27):
-        offset = tap_offsets[tap_index]
-        moved = shifted(hidden_one, offset).reshape(-1, channels)
-        grad_two.append(jnp.dot(moved.T, delta_two, preferred_element_type=jnp.float32) * scale_two)
-        mirror = (-offset[0], -offset[1], -offset[2])
-        back_one = back_one + jnp.dot(
-            shifted(delta_grid, mirror).reshape(-1, channels),
-            k_second[tap_index].T,
-            preferred_element_type=jnp.float32,
+        errors.append(error)
+    outer = errors[0] * w_out[0:1, :] + errors[1] * w_out[1:2, :]
+    delta_three = (outer * scale_dense * (gate * (1.0 + third * (1.0 - gate)))).astype(jnp.bfloat16)
+    delta_ref[...] = delta_three
+    for j in range(8):
+        back = matmul(delta_three, w_vmem[j * 256 : j * 256 + 256, :], ((1,), (1,)))
+        for i in range(4):
+            pooled[j // 2, (j % 2) * 4 + i] = back[:, i * 64 : i * 64 + 64]
+    spread = (pooled[...] * (scale_dense * 0.25)).reshape(2, 1, 2, 1, 8 * batch, 64)
+    spread = jnp.broadcast_to(spread, (2, 2, 2, 2, 8 * batch, 64)).reshape(points, 64)
+    delta = (spread * silu_slope(pre_two[...])).astype(jnp.bfloat16).astype(jnp.float32)
+    mid_pad[1:5, 1:5] = delta.astype(jnp.bfloat16).reshape(4, 4, 8 * batch, 64)
+    delta3 = z_shifts(delta.reshape(16, 8, batch, 64), -1)
+    del_pad[1:5, 1:5] = delta3.astype(jnp.bfloat16).reshape(4, 4, 8 * batch, 192)
+    total = jnp.zeros((points, 64), jnp.float32)
+    for pair in range(9):
+        first_off, second_off = 1 - pair // 3, 1 - pair % 3
+        grad_two_ref[pair] = (
+            matmul(hidden_t, window(mid_pad, first_off, second_off)) * scale_two
         )
-    delta_one = (back_one * scale_two * silu_slope(pre_one)).astype(jnp.bfloat16)
-    grad_one = jnp.dot(columns.T, delta_one, preferred_element_type=jnp.float32) * scale_one
-    return (pred, grad_one, jnp.stack(grad_two), grad_out, features, delta_three)
+        total = total + matmul(
+            window(del_pad, first_off, second_off), k_back[pair], ((1,), (1,))
+        )
+    pre_one[...] = total * scale_two * silu_slope(pre_one[...])
+    delta_one = jnp.concatenate(
+        [pre_one[pl.ds(slot, 128, stride=batch), :] for slot in range(batch)], axis=0
+    ).astype(jnp.bfloat16)
+    grad_one_ref[...] = matmul(columns, delta_one) * scale_one
+
+
+def forward_back(rows, aims, valid, k_first, k_second, w_hidden, w_out):
+    batch = rows.shape[0]
+    k_pairs = k_second.reshape(9, 192, 64)
+    k_back = k_second.reshape(9, 3, 64, 64).transpose(0, 2, 1, 3).reshape(9, 64, 192)
+    vmem = pl.BlockSpec(memory_space=pltpu.VMEM)
+    return pl.pallas_call(
+        network,
+        out_shape=(
+            jax.ShapeDtypeStruct((batch, 2), jnp.float32),
+            jax.ShapeDtypeStruct((64, 64), jnp.float32),
+            jax.ShapeDtypeStruct((9, 192, 64), jnp.float32),
+            jax.ShapeDtypeStruct((2, 2048), jnp.float32),
+            jax.ShapeDtypeStruct((batch, 2048), jnp.bfloat16),
+            jax.ShapeDtypeStruct((batch, 2048), jnp.bfloat16),
+        ),
+        in_specs=[vmem] * 6 + [pl.BlockSpec(memory_space=pl.ANY), vmem],
+        out_specs=(vmem,) * 6,
+        scratch_shapes=[
+            pltpu.VMEM((2048, 2048), jnp.bfloat16),
+            pltpu.VMEM((64 * batch, 128), jnp.float32),
+            pltpu.VMEM((128 * batch, 64), jnp.float32),
+            pltpu.VMEM((6, 6, 8 * batch, 192), jnp.bfloat16),
+            pltpu.VMEM((6, 6, 8 * batch, 192), jnp.bfloat16),
+            pltpu.VMEM((6, 6, 8 * batch, 64), jnp.bfloat16),
+            pltpu.VMEM((128 * batch, 64), jnp.float32),
+            pltpu.VMEM((4, 8, batch, 64), jnp.float32),
+            pltpu.SemaphoreType.DMA,
+        ],
+        compiler_params=pltpu.CompilerParams(vmem_limit_bytes=48 * 1024 * 1024),
+    )(
+        rows, aims, valid, jnp.pad(k_first, ((0, 10), (0, 0))), k_pairs, k_back, w_hidden,
+        w_out.T.astype(jnp.float32),
+    )
 
 
 def row_update(weight, grad):
@@ -230,14 +321,16 @@
         jnp.bfloat16
     )
     send_valid = jnp.sum(select, axis=1).astype(jnp.bfloat16)
-    recv_rows, recv_aims, recv_valid = (
-        lax.all_to_all(send_rows, "wall", split_axis=0, concat_axis=0, tiled=True),
-        lax.all_to_all(send_aims, "wall", split_axis=0, concat_axis=0, tiled=True),
-        lax.all_to_all(send_valid, "wall", split_axis=0, concat_axis=0, tiled=True),
-    )
+    parcel = jnp.concatenate(
+        [send_rows, send_aims, send_valid[:, None], jnp.zeros((select.shape[0], 125), jnp.bfloat16)], axis=1
+    )
+    parcel = lax.all_to_all(parcel, "wall", split_axis=0, concat_axis=0, tiled=True)
+    tail = parcel[:, 256:259].astype(jnp.float32)
     pred, grad_one, grad_two, grad_out, features, delta_three = forward_back(
-        recv_rows, recv_aims, recv_valid, k_first[0], k_second[0], w_hidden[0], w_out[0]
-    )
+        parcel[:, :256], tail[:, 0:2], tail[:, 2:3], k_first[0], k_second[0], w_hidden[0], w_out[0]
+    )
+    grad_one = grad_one[:54]
+    grad_two = grad_two.reshape(27, 64, 64)
     back = lax.all_to_all(pred, "wall", split_axis=0, concat_axis=0, tiled=True)
     stress_local = jnp.dot(select.T, back, precision=highest)
     stress = stress_local.T[:, None, :]
@@ -257,7 +350,7 @@
     grad_one, grad_two, grad_out = lax.psum((grad_one, grad_two, grad_out), "stream")
     new_k_second = row_update(k_second[0], grad_two)
     new_k_first = row_update(k_first[0], grad_one)
-    new_w_out = whole_update(w_out[0], grad_out)
+    new_w_out = whole_update(w_out[0], grad_out.T)
     return (new_field, stress, new_k_first[None], new_k_second[None], new_w_hidden, new_w_out[None])
 
 

time: 255 us -> 136 us (0.53)
  local copies, waits for them, and re-layouts: 79.9 us -> 15.1 us
  matrix products: 58.8 us -> 7.75 us
  blocking collectives: 58.2 us -> 43.7 us
  Pallas kernels: 0 us -> 14.1 us
    dot_general x87 -> x0, matrix products: 52.4 us -> none  [the longest x27 22.9 us: forward_back(): jnp.dot(moved.T, delta_two, preferred_element_type=jnp.float32) * scale_two]
    slice x32 -> x3, local copies, waits for them, and re-layouts: 50.6 us -> 0.08 us  [the longest x1 0.07 us: body(): tail[:, 2:3]]
    pallas_call x0 -> x1, Pallas kernels: none -> 14.1 us  [forward_back(): pl.pallas_call(network, out_shape=(jax.ShapeDtypeStruct((batch, 2), jnp.f...]
    all_to_all x2 -> x0, blocking collectives: 14 us -> none  [the longest x1 7 us: body(): back = lax.all_to_all(pred, 'wall', split_axis=0, concat_axis=0, tiled=True)]
    concatenate x1 -> x3, local copies, waits for them, and re-layouts: 6.41 us -> 0.75 us  [body(): jnp.concatenate([send_rows, send_aims, send_valid[:, None], jnp.zeros((se...]
    unnamed x212 -> x34, local copies, waits for them, and re-layouts: 6.51 us -> 2.07 us
    all_to_all x1, waiting for transfers between devices: 0.01 us -> 3.75 us  [body(): lax.all_to_all(features, 'stream', split_axis=1, concat_axis=0, tiled=True)]
    ppermute x2, starting transfers between devices: 2.93 us -> 6.15 us  [with_halo(): after = lax.ppermute(first, axis, down)]
  transfers between devices with their start and end apart: 8 -> 8, of which waited for: 1 -> 2; matrix products, arithmetic and copies ran while one was open for 56% -> 20% of each run, Pallas kernels for 0% -> 10%
where the time goes in v1:
time: 136 us; the launch traced here: 135 us
  blocking collectives  43.7 us (32%)
  other arithmetic  17.3 us (13%)
  starting transfers between devices  16.9 us (12%)
  local copies, waits for them, and re-layouts  15.1 us (11%)
  between operations  15.1 us (11%)
  Pallas kernels  14.1 us (10%)
  matrix products  7.75 us (6%)
  waiting for transfers between devices  5.22 us (4%)
    psum x1, blocking collectives, body(): lax.psum((grad_one, grad_two, grad_out), 'stream')  28.9 us
    all_gather x1, blocking collectives, body(): lax.all_gather(delta_three, 'stream', axis=0, tiled=True)  14.8 us
    pallas_call x1, Pallas kernels, forward_back(): pl.pallas_call(network, out_shape=(jax.ShapeDtypeStruct((batch, 2), jnp.f...  14.1 us
    ppermute x2, starting transfers between devices, with_halo(): after = lax.ppermute(first, axis, down)  6.15 us
    all_to_all x1, starting transfers between devices, body(): lax.all_to_all(parcel, 'wall', split_axis=0, concat_axis=0, tiled=True)  4.19 us
    all_to_all x1, waiting for transfers between devices, body(): lax.all_to_all(features, 'stream', split_axis=1, concat_axis=0, tiled=True)  3.75 us
    all_to_all x1, starting transfers between devices, body(): lax.all_to_all(features, 'stream', split_axis=1, concat_axis=0, tiled=True)  3.32 us
    all_to_all x1, starting transfers between devices, body(): back = lax.all_to_all(pred, 'wall', split_axis=0, concat_axis=0, tiled=True)  3.25 us
  transfers between devices with their start and end apart: 8, of which 2 were waited for; matrix products, arithmetic and copies ran while one was open for 20% of the time, Pallas kernels for 10%

profile of v1, /device:TPU:0, one launch (start us, length us, event | category | flops | bytes accessed | tf_op | source)
XLA Modules:
  0.0 135.2 jit_solution(16262269947585768224)
XLA Ops:
  7.2 1.4 %fusion.32 = (f32[3,1,16,128]{3,2,1,0:T(8,128)}, f32[3,1,16,128]{3,2,1,0:T(8,128)}) fusion(f32[3,8,16,128]{3,2,1,0:T(8,128)} %param.18), kind=kLoop, calls=%fused_computation.81 | loop fusion | bytes 98304 | tf_op jit(solution)/shard_map/slice | solution.py:39
  8.5 3.9 %collective-permute-start.1 = (f32[3,1,16,128]{3,2,1,0:T(8,128)}, f32[3,1,16,128]{3,2,1,0:T(8,128)}, u32[]{:S(2)}, u32[]{:S(2)}) collective-permute-start(f32[3,1,16,128]{3,2,1,0:T(8,128)} %get-tuple-element.101), channel_id=1, source_target_pairs={{8,0},{16,8},{24,16},{0,24},{9,1},{17,9},{25,17},{1,25},{10,2},{18... | collective-permute-start | bytes 73736 | tf_op jit(solution)/shard_map/ppermute | solution.py:41
  13.8 0.9 fusion.30
  14.7 1.6 %slice_bitcast_fusion.2 = (f32[8,16,128]{2,1,0:T(8,128)S(1)}, f32[8,16,128]{2,1,0:T(8,128)}, f32[8,16,128]{2,1,0:T(8,128)}) fusion(f32[3,8,16,128]{3,2,1,0:T(8,128)} %param.18), kind=kLoop, calls=%fused_computation.77 | loop fusion | bytes 393216 | tf_op jit(solution)/shard_map/mul | solution.py:302
  16.2 0.7 fusion.19
  17.0 0.8 select_reduce_fusion
  18.5 0.7 convert_bitcast_fusion.w_out
  19.2 1.4 %convolution_bitcast_fusion.1 = f32[3,8,32,128]{3,2,1,0:T(8,128)S(1)} fusion(f32[32,16,1,1]{0,1,3,2:T(8,128)} %constant.219, f32[3,8,16,128]{3,2,1,0:T(8,128)} %param.18), kind=kOutput, calls=%fused_computation.6 | convolution fusion | flops 18874368 | bytes 591872 | tf_op jit(solution)/shard_map/cyxz,wx->cywz/dot_general | solution.py:290
  20.7 1.6 %fusion.8 = f32[16,3,16,128]{3,0,2,1:T(8,128)S(1)} fusion(f32[16,8,1,1]{0,1,3,2:T(8,128)} %constant.220, f32[3,8,16,128]{3,2,1,0:T(8,128)} %param.18), kind=kOutput, calls=%fused_computation.22 | convolution fusion | flops 9437184 | bytes 590336 | tf_op jit(solution)/shard_map/cyxz,wy->cwxz/dot_general | solution.py:281
  22.3 2.2 %convolution_bitcast_fusion = f32[3,8,16,256]{3,2,1,0:T(8,128)} fusion(f32[256,128,1,1]{1,0,3,2:T(8,128)} %constant.221, f32[3,8,16,128]{3,2,1,0:T(8,128)} %param.18), kind=kOutput, calls=%fused_computation.5 | convolution fusion | flops 150994944 | bytes 720896 | tf_op jit(solution)/shard_map/cyxz,wz->cyxw/dot_general | solution.py:299
  24.5 1.2 reshape.272
  29.2 0.7 constant_dynamic-update-slice_fusion.2
  30.0 0.7 constant_dynamic-update-slice_fusion
  30.7 0.7 copy-done.11
  32.7 2.1 %reshape.275 = f32[2,2,4,4,4,16,8]{6,5,4,3,2,1,0:T(8,128)S(1)} reshape(f32[2,8,16,128]{3,2,1,0:T(8,128)} %pad_maximum_fusion.1) | data formatting | bytes 262144 | tf_op jit(solution)/shard_map/reshape | solution.py:307
  35.9 0.9 convolution_convert_fusion.1
  36.9 1.4 %maximum_maximum_fusion = bf16[4,2,384]{2,1,0:T(2,128)(2,1)} fusion(bf16[4,2,1]{2,1,0:T(2,128)(2,1)S(1)} %convert_element_type.98, bf16[4,2,2]{2,1,0:T(2,128)(2,1)S(1)} %bitcast.106, bf16[4,2,256]{2,1,0:T(2,128)(2,1)S(1)} %concatenate.20, bf16[384]{0:T(512)(128)(2,1)} %pad.16.clone), kind=kLoop, calls=%fused_computation.48 | loop fusion | flops 24576 | bytes 11056 | tf_op jit(solution)/shard_map/concatenate | solution.py:324
  38.3 4.2 %all-to-all-start = ((bf16[4,2,384]{2,1,0:T(2,128)(2,1)}), bf16[4,2,384]{2,1,0:T(2,128)(2,1)S(1)}, u32[]{:S(2)}, u32[]{:S(2)}) async-start(bf16[4,2,384]{2,1,0:T(2,128)(2,1)} %maximum_maximum_fusion), calls=%async_computation | async-start | bytes 12288 | tf_op jit(solution)/shard_map/all_to_all | solution.py:327
  42.5 1.0 fusion.29
  43.5 2.3 %collective-permute-start.3 = (f32[3,10,1,128]{3,2,1,0:T(1,128)S(1)}, f32[3,10,1,128]{3,2,1,0:T(1,128)S(1)}, u32[]{:S(2)}, u32[]{:S(2)}) collective-permute-start(f32[3,10,1,128]{3,2,1,0:T(1,128)S(1)} %get-tuple-element.92), channel_id=1, source_target_pairs={{1,0},{2,1},{3,2},{4,3},{5,4},{6,5},{7,6},{0,7},{9,8},{10,9},{11,1... | collective-permute-start | bytes 46088 | tf_op jit(solution)/shard_map/ppermute | solution.py:41
  45.7 1.4 %all-to-all-done = bf16[4,2,384]{2,1,0:T(2,128)(2,1)S(1)} async-done(((bf16[4,2,384]{2,1,0:T(2,128)(2,1)}), bf16[4,2,384]{2,1,0:T(2,128)(2,1)S(1)}, u32[]{:S(2)}, u32[]{:S(2)}) %all-to-all-start) | async-done | bytes 6176 | tf_op jit(solution)/shard_map/all_to_all | solution.py:327
  47.3 14.1 %shard_map.145 = (f32[8,2]{1,0:T(8,128)S(1)}, f32[64,64]{1,0:T(8,128)S(1)}, f32[9,192,64]{2,1,0:T(8,128)}, f32[2,2048]{1,0:T(2,128)S(1)}, bf16[8,2048]{1,0:T(8,128)(2,1)}, /*index=5*/bf16[8,2048]{1,0:T(8,128)(2,1)S(1)}) custom-call(bf16[8,256]{1,0:T(8,128)(2,1)S(1)} %slice.224.rows, f32[8,2]{1,0:T(8,128)S(1)} %bitcast.96, f32[8,1]{1,0:T(8,128)S(1)} %slice.202.valid, ...), custom_call_target="tpu_custom_call" | custom-call | tf_op jit(solution)/shard_map/pallas_call | solution.py:225
  62.1 3.3 %all-to-all-start.1 = ((f32[4,2,2]{1,2,0:T(2,128)}), f32[4,2,2]{1,2,0:T(2,128)S(1)}, u32[]{:S(2)}, u32[]{:S(2)}) async-start(f32[4,2,2]{1,2,0:T(2,128)} %copy.60), calls=%async_computation.1 | async-start | bytes 8192 | tf_op jit(solution)/shard_map/all_to_all | solution.py:334
  65.4 28.9 %all-reduce.1 = (f32[54,64]{1,0:T(8,128)S(1)}, f32[2,2048]{1,0:T(2,128)S(1)}) all-reduce(f32[54,64]{1,0:T(8,128)S(1)} %slice.203, f32[2,2048]{1,0:T(2,128)S(1)} %get-tuple-element.65), channel_id=1, replica_groups=mesh['wall'=4,'stream'=8] {'stream'}, use_global_device_ids=true, to_apply=%region_4.0 | all-reduce | flops 7552 | bytes 60416 | tf_op jit(solution)/shard_map/psum | solution.py:350
  97.1 14.8 %all_gather.3 = bf16[64,2048]{1,0:T(8,128)(2,1)S(1)} all-gather(bf16[8,2048]{1,0:T(8,128)(2,1)S(1)} %get-tuple-element.64), channel_id=1, replica_groups=mesh['wall'=4,'stream'=8] {'stream'}, dimensions={0}, use_global_device_ids=true | all-gather | bytes 294912 | tf_op jit(solution)/shard_map/all_gather | solution.py:343
  111.9 3.3 %all-to-all-start.2 = ((bf16[8,8,256]{2,0,1:T(8,128)(2,1)}), bf16[8,8,256]{2,0,1:T(8,128)(2,1)S(1)}, u32[]{:S(2)}, u32[]{:S(2)}) async-start(bf16[8,8,256]{2,0,1:T(8,128)(2,1)} %bitcast.36), calls=%async_computation.2 | async-start | bytes 65536 | tf_op jit(solution)/shard_map/all_to_all | solution.py:339
  115.3 0.8 fusion.18
  116.3 0.8 fusion.5
  117.1 3.8 %all-to-all-done.2 = bf16[8,8,256]{2,0,1:T(8,128)(2,1)S(1)} async-done(((bf16[8,8,256]{2,0,1:T(8,128)(2,1)}), bf16[8,8,256]{2,0,1:T(8,128)(2,1)S(1)}, u32[]{:S(2)}, u32[]{:S(2)}) %all-to-all-start.2) | async-done | bytes 32800 | tf_op jit(solution)/shard_map/all_to_all | solution.py:339
  121.4 3.0 %fusion = f32[1,256,2048]{2,1,0:T(8,128)} fusion(f32[256,2048]{1,0:T(8,128)S(1)} %get-tuple-element.108, f32[256]{0:T(256)S(1)} %add_sqrt_fusion.1, bf16[1,2048,2048]{2,1,0:T(8,128)(2,1)} %param.23, s32[]{:T(128)S(6)} %select_n.33), kind=kLoop, calls=%fused_computation.3 | loop fusion | flops 2097152 | bytes 5243908 | tf_op jit(solution)/shard_map/broadcast_in_dim | solution.py:349
  124.5 1.5 %multiply_reduce_fusion.1 = f32[27,64]{1,0:T(8,128)S(1)} fusion(f32[27,64,64]{2,1,0:T(8,128)} %all-reduce.4.cloned.1.call-done), kind=kLoop, calls=%fused_computation.11 | loop fusion | flops 219456 | bytes 449280 | tf_op jit(solution)/shard_map/reduce_sum | solution.py:256
  126.0 2.4 %fusion.1 = f32[1,27,64,64]{3,2,1,0:T(8,128)} fusion(f32[27,64,64]{2,1,0:T(8,128)} %all-reduce.4.cloned.1.call-done, bf16[1,27,64,64]{3,2,1,0:T(8,128)(2,1)S(1)} %copy-done, f32[27,64]{1,0:T(8,128)S(1)} %add_sqrt_fusion), kind=kLoop, calls=%fused_computation.10 | loop fusion | flops 442368 | bytes 1112832 | tf_op jit(solution)/shard_map/broadcast_in_dim | solution.py:354
  (93 shorter events, 11.7 us)
Async XLA Ops:
  8.5 21.4 %collective-permute-start.1 = (f32[3,1,16,128]{3,2,1,0:T(8,128)}, f32[3,1,16,128]{3,2,1,0:T(8,128)}, u32[]{:S(2)}, u32[]{:S(2)}) collective-permute-start(f32[3,1,16,128]{3,2,1,0:T(8,128)} %get-tuple-element.101), channel_id=1, source_target_pairs={{8,0},{16,8},{24,16},{0,24},{9,1},{17,9},{25,17},{1,25},{10,2},{18... | collective-permute-start | bytes 73736 | tf_op jit(solution)/shard_map/ppermute | solution.py:41
  12.4 16.7 %collective-permute-start = (f32[3,1,16,128]{3,2,1,0:T(8,128)}, f32[3,1,16,128]{3,2,1,0:T(8,128)}, u32[]{:S(2)}, u32[]{:S(2)}) collective-permute-start(f32[3,1,16,128]{3,2,1,0:T(8,128)} %get-tuple-element.102), channel_id=1, source_target_pairs={{0,8},{8,16},{16,24},{24,0},{1,9},{9,17},{17,25},{25,1},{2,10},{10... | collective-permute-start | bytes 73736 | tf_op jit(solution)/shard_map/ppermute | solution.py:40
  13.1 14.3 %copy-start.15 = (pred[4]{0:T(512)(128)(4,1)}, pred[4]{0:T(512)(128)(4,1)S(1)}, u32[]{:S(2)}) copy-start(pred[4]{0:T(512)(128)(4,1)S(1)} %compare_and_fusion) | copy-start | bytes 16
  18.5 9.2 %copy-start.13 = (s32[4]{0:T(128)}, s32[4]{0:T(128)S(1)}, u32[]{:S(2)}) copy-start(s32[4]{0:T(128)S(1)} %multiply_add_fusion) | copy-start | bytes 52
  18.5 8.3 %copy-start.12 = (s32[1024]{0:T(1024)}, s32[1024]{0:T(1024)S(1)}, u32[]{:S(2)}) copy-start(s32[1024]{0:T(1024)S(1)} %pad_clamp_fusion) | copy-start | bytes 12292
  20.7 7.2 %copy-start.2 = (f32[3,8,32,128]{3,2,1,0:T(8,128)}, f32[3,8,32,128]{3,2,1,0:T(8,128)S(1)}, u32[]{:S(2)}) copy-start(f32[3,8,32,128]{3,2,1,0:T(8,128)S(1)} %convolution_bitcast_fusion.1) | copy-start | bytes 1179652
  25.7 2.3 %copy-start = (bf16[1,27,64,64]{3,2,1,0:T(8,128)(2,1)S(1)}, bf16[1,27,64,64]{3,2,1,0:T(8,128)(2,1)}, u32[]{:S(2)}) copy-start(bf16[1,27,64,64]{3,2,1,0:T(8,128)(2,1)} %param.22) | copy-start | bytes 663556
  26.3 2.2 %copy-start.9 = (bf16[1,54,64]{2,1,0:T(8,128)(2,1)S(1)}, bf16[1,54,64]{2,1,0:T(8,128)(2,1)}, u32[]{:S(2)}) copy-start(bf16[1,54,64]{2,1,0:T(8,128)(2,1)} %param.21) | copy-start | bytes 20740
  26.3 3.6 %copy-start.1 = (f32[3,8,16,128]{3,2,1,0:T(8,128)S(1)}, f32[3,8,16,128]{3,2,1,0:T(8,128)}, u32[]{:S(2)}) copy-start(f32[3,8,16,128]{3,2,1,0:T(8,128)} %param.18) | copy-start | bytes 589828
  30.7 0.7 copy-start.11
  31.4 0.7 copy-start.5
  38.3 8.9 %all-to-all-start = ((bf16[4,2,384]{2,1,0:T(2,128)(2,1)}), bf16[4,2,384]{2,1,0:T(2,128)(2,1)S(1)}, u32[]{:S(2)}, u32[]{:S(2)}) async-start(bf16[4,2,384]{2,1,0:T(2,128)(2,1)} %maximum_maximum_fusion), calls=%async_computation | async-start | bytes 12288 | tf_op jit(solution)/shard_map/all_to_all | solution.py:327
  42.5 82.0 %all-reduce.4.cloned.1.call-start = ((), (), s32[]{:S(2)}) async-start(), calls=%async_computation.3 | async-start | bytes 1769472 | tf_op jit(solution)/shard_map/psum | solution.py:350
  43.5 72.7 %collective-permute-start.3 = (f32[3,10,1,128]{3,2,1,0:T(1,128)S(1)}, f32[3,10,1,128]{3,2,1,0:T(1,128)S(1)}, u32[]{:S(2)}, u32[]{:S(2)}) collective-permute-start(f32[3,10,1,128]{3,2,1,0:T(1,128)S(1)} %get-tuple-element.92), channel_id=1, source_target_pairs={{1,0},{2,1},{3,2},{4,3},{5,4},{6,5},{7,6},{0,7},{9,8},{10,9},{11,1... | collective-permute-start | bytes 46088 | tf_op jit(solution)/shard_map/ppermute | solution.py:41
  45.7 70.3 %collective-permute-start.2 = (f32[3,10,1,128]{3,2,1,0:T(1,128)S(1)}, f32[3,10,1,128]{3,2,1,0:T(1,128)S(1)}, u32[]{:S(2)}, u32[]{:S(2)}) collective-permute-start(f32[3,10,1,128]{3,2,1,0:T(1,128)S(1)} %get-tuple-element.93), channel_id=1, source_target_pairs={{0,1},{1,2},{2,3},{3,4},{4,5},{5,6},{6,7},{7,0},{8,9},{9,10},{10,1... | collective-permute-start | bytes 46088 | tf_op jit(solution)/shard_map/ppermute | solution.py:40
  47.3 49.2 %copy-start.10 = (bf16[1,2048,2]{1,2,0:T(2,128)(2,1)S(1)}, bf16[1,2048,2]{1,2,0:T(2,128)(2,1)}, u32[]{:S(2)}) copy-start(bf16[1,2048,2]{1,2,0:T(2,128)(2,1)} %param.24) | copy-start | bytes 24580
  47.3 68.0 %copy-start.14 = (s32[4]{0:T(128)S(1)}, s32[4]{0:T(128)}, u32[]{:S(2)}) copy-start(s32[4]{0:T(128)} %copy-done.13) | copy-start | bytes 52
  47.3 68.8 %copy-start.3 = (f32[3,8,32,128]{3,2,1,0:T(8,128)S(1)}, f32[3,8,32,128]{3,2,1,0:T(8,128)}, u32[]{:S(2)}) copy-start(f32[3,8,32,128]{3,2,1,0:T(8,128)} %copy-done.2) | copy-start | bytes 1179652
  47.3 68.8 %slice-start = ((f32[3,8,32,128]{3,2,1,0:T(8,128)}), f32[3,8,16,128]{3,2,1,0:T(8,128)S(1)}, s32[]{:S(2)}) async-start(f32[3,8,32,128]{3,2,1,0:T(8,128)} %copy-done.2), calls=%async_computation.4 | async-start | bytes 393216 | tf_op jit(solution)/shard_map/slice | solution.py:292
  47.3 69.0 %copy-start.4 = (f32[3,8,16,256]{3,2,1,0:T(8,128)S(1)}, f32[3,8,16,256]{3,2,1,0:T(8,128)}, u32[]{:S(2)}) copy-start(f32[3,8,16,256]{3,2,1,0:T(8,128)} %convolution_bitcast_fusion) | copy-start | bytes 1179652
  47.3 69.0 %copy-start.6 = (f32[3,8,16,128]{3,2,1,0:T(8,128)S(1)}, f32[3,8,16,128]{3,2,1,0:T(8,128)}, u32[]{:S(2)}) copy-start(f32[3,8,16,128]{3,2,1,0:T(8,128)} %copy-done.5) | copy-start | bytes 589828
  47.3 69.0 %copy-start.7 = (f32[8,16,128]{2,1,0:T(8,128)S(1)}, f32[8,16,128]{2,1,0:T(8,128)}, u32[]{:S(2)}) copy-start(f32[8,16,128]{2,1,0:T(8,128)} %get-tuple-element.99) | copy-start | bytes 196612
  47.3 69.0 %copy-start.8 = (f32[8,16,128]{2,1,0:T(8,128)S(1)}, f32[8,16,128]{2,1,0:T(8,128)}, u32[]{:S(2)}) copy-start(f32[8,16,128]{2,1,0:T(8,128)} %get-tuple-element.100) | copy-start | bytes 196612
  62.1 49.7 %all-to-all-start.1 = ((f32[4,2,2]{1,2,0:T(2,128)}), f32[4,2,2]{1,2,0:T(2,128)S(1)}, u32[]{:S(2)}, u32[]{:S(2)}) async-start(f32[4,2,2]{1,2,0:T(2,128)} %copy.60), calls=%async_computation.1 | async-start | bytes 8192 | tf_op jit(solution)/shard_map/all_to_all | solution.py:334
  111.9 9.0 %all-to-all-start.2 = ((bf16[8,8,256]{2,0,1:T(8,128)(2,1)}), bf16[8,8,256]{2,0,1:T(8,128)(2,1)S(1)}, u32[]{:S(2)}, u32[]{:S(2)}) async-start(bf16[8,8,256]{2,0,1:T(8,128)(2,1)} %bitcast.36), calls=%async_computation.2 | async-start | bytes 65536 | tf_op jit(solution)/shard_map/all_to_all | solution.py:339
Sparse Core Ops, SparseCore 0:
  62.2 57.5 all-reduce.3

commit v2 on v1

--- a/solution.py
+++ b/solution.py
@@ -1,3 +1,4 @@
+import functools
 import math
 
 import jax
@@ -13,7 +14,6 @@
 PX = 4
 PZ = 8
 CAP = 2
-FEATS = 2048
 
 
 highest = lax.Precision.HIGHEST
@@ -121,13 +121,54 @@
     return lax.dot_general(left, right, (dims, ((), ())), preferred_element_type=jnp.float32)
 
 
+def remote(source, target, semaphores, row, hop, axis, peer):
+    return pltpu.make_async_remote_copy(
+        src_ref=source, dst_ref=target,
+        send_sem=semaphores.at[row, hop], recv_sem=semaphores.at[row + 1, hop],
+        device_id={axis: peer}, device_id_type=pl.DeviceIdType.MESH,
+    )
+
+
+def head(third, w_out, tail):
+    scale_dense = 1.0 / math.sqrt(2048.0)
+    gate = sigmoid(third)
+    hidden = (third * gate).astype(jnp.bfloat16).astype(jnp.float32)
+    preds, errors, sums = [], [], []
+    for i in range(2):
+        pred = jnp.sum(hidden * w_out[i : i + 1, :], axis=1, keepdims=True) * scale_dense
+        error = tail[:, 2:3] * (pred - tail[:, i : i + 1])
+        sums.append(jnp.sum(hidden * error, axis=0, keepdims=True) * scale_dense)
+        preds.append(pred)
+        errors.append(error)
+    outer = errors[0] * w_out[0:1, :] + errors[1] * w_out[1:2, :]
+    delta = (outer * scale_dense * (gate * (1.0 + third * (1.0 - gate)))).astype(jnp.bfloat16)
+    return preds, sums, delta
+
+
 def network(
-    rows, aims, valid, k_first, k_second, k_back, w_hbm, w_out,
-    pred_ref, grad_one_ref, grad_two_ref, grad_out_ref, feat_ref, delta_ref,
-    w_vmem, cols, pre_one, hid_pad, del_pad, mid_pad, pre_two, pooled, w_sem,
+    n, walls, per, parcel, k_first, k_second, k_back, w_hbm, w_out,
+    back_ref, new_first, new_second, new_hidden, new_out,
+    w_vmem, cols, pre_one, hid_pad, del_pad, mid_pad, pre_two, pooled,
+    feat_in, tail_in, feat_all, delta_all, grads, grads_in, update, pred_in,
+    w_sem, sems, wall_sems,
 ):
-    batch = rows.shape[0]
+    me, wall = lax.axis_index("stream"), lax.axis_index("wall")
+    barrier = pltpu.get_barrier_semaphore()
+    for hop in range(1, n):
+        pl.semaphore_signal(
+            barrier, inc=1, device_id={"stream": lax.rem(me + hop, n)},
+            device_id_type=pl.DeviceIdType.MESH,
+        )
+    for hop in range(1, walls):
+        pl.semaphore_signal(
+            barrier, inc=1, device_id={"wall": lax.rem(wall + hop, walls)},
+            device_id_type=pl.DeviceIdType.MESH,
+        )
+    batch = parcel.shape[0]
     points = 128 * batch
+    share = 2048 // n
+    tail = parcel[:, 256:384].astype(jnp.float32)
+    rows = parcel[:, 0:256].astype(jnp.float32)
     fetch = pltpu.make_async_copy(w_hbm, w_vmem, w_sem)
     fetch.start()
     scale_one = 1.0 / math.sqrt(54.0)
@@ -139,7 +180,7 @@
     lane = lax.broadcasted_iota(jnp.int32, (batch, 128), 1)
     at = (lane // 32, (lane // 8) % 4, lane % 8)
     cols[54 * batch : 64 * batch, :] = jnp.zeros((10 * batch, 128), jnp.float32)
-    channel = [rows[:, 0:128].astype(jnp.float32), rows[:, 128:256].astype(jnp.float32)]
+    channel = [rows[:, 0:128], rows[:, 128:256]]
     for tap, offset in enumerate(tap_offsets):
         inside = None
         for place, step, size in zip(at, offset, (4, 4, 8)):
@@ -165,32 +206,42 @@
     hid_pad[1:5, 1:5] = hidden3.astype(jnp.bfloat16).reshape(4, 4, 8 * batch, 192)
     total = jnp.zeros((points, 64), jnp.float32)
     for pair in range(9):
-        total = total + matmul(window(hid_pad, pair // 3 - 1, pair % 3 - 1), k_second[pair])
+        total = total + matmul(window(hid_pad, pair // 3 - 1, pair % 3 - 1), k_second[pair * 192 : pair * 192 + 192, :])
     second = total * scale_two
     pre_two[...] = second
     act = (second * sigmoid(second)).reshape(2, 2, 2, 2, 8 * batch, 64)
     pool = (act[:, 0, :, 0] + act[:, 0, :, 1] + act[:, 1, :, 0] + act[:, 1, :, 1]) * 0.25
     pieces = pool.reshape(32, batch, 64)
-    features = jnp.concatenate([pieces[i] for i in range(32)], axis=1).astype(jnp.bfloat16)
-    feat_ref[...] = features
+    features = jnp.concatenate([pieces[i] for i in range(32)], axis=1)
+    feat_in[0] = jnp.concatenate([features[:, :1024], features[:, 1024:]], axis=0).astype(
+        jnp.bfloat16
+    )
+    tail_in[0] = tail
+    features = features.astype(jnp.bfloat16)
+    pl.semaphore_wait(barrier, n + walls - 2)
+    copies = []
+    for hop in range(1, n):
+        peer = lax.rem(me + hop, n)
+        copies.append(remote(feat_in.at[0], feat_in.at[hop], sems, 0, hop, "stream", peer))
+        copies.append(remote(tail_in.at[0], tail_in.at[hop], sems, 2, hop, "stream", peer))
+    for copy in copies:
+        copy.start()
     fetch.wait()
-    third = jnp.concatenate(
-        [matmul(features, w_vmem[:, j * 512 : j * 512 + 512]) for j in range(4)], axis=1
-    ) * scale_dense
-    gate = sigmoid(third)
-    hidden_three = (third * gate).astype(jnp.bfloat16).astype(jnp.float32)
-    errors = []
-    for i in range(2):
-        pred = jnp.sum(hidden_three * w_out[i : i + 1, :], axis=1, keepdims=True) * scale_dense
-        pred_ref[:, i : i + 1] = pred
-        error = valid[...] * (pred - aims[:, i : i + 1])
-        grad_out_ref[i : i + 1, :] = (
-            jnp.sum(hidden_three * error, axis=0, keepdims=True) * scale_dense
-        )
-        errors.append(error)
-    outer = errors[0] * w_out[0:1, :] + errors[1] * w_out[1:2, :]
-    delta_three = (outer * scale_dense * (gate * (1.0 + third * (1.0 - gate)))).astype(jnp.bfloat16)
-    delta_ref[...] = delta_three
+
+    def dense(values):
+        return jnp.concatenate(
+            [matmul(values, w_vmem[:, j * 512 : j * 512 + 512]) for j in range(4)], axis=1
+        ) * scale_dense
+
+    preds, _, delta_three = head(dense(features), w_out, tail)
+    lane_out = lax.broadcasted_iota(jnp.int32, (batch, 128), 1)
+    pred_in[0] = jnp.where(lane_out == 0, preds[0], jnp.where(lane_out == 1, preds[1], 0.0))
+    returns = []
+    for hop in range(1, walls):
+        peer = lax.rem(wall + hop, walls)
+        returns.append(remote(pred_in.at[0], pred_in.at[hop], wall_sems, 0, hop, "wall", peer))
+    for copy in returns:
+        copy.start()
     for j in range(8):
         back = matmul(delta_three, w_vmem[j * 256 : j * 256 + 256, :], ((1,), (1,)))
         for i in range(4):
@@ -204,9 +255,17 @@
     total = jnp.zeros((points, 64), jnp.float32)
     for pair in range(9):
         first_off, second_off = 1 - pair // 3, 1 - pair % 3
-        grad_two_ref[pair] = (
-            matmul(hidden_t, window(mid_pad, first_off, second_off)) * scale_two
+        grad_two = (matmul(hidden_t, window(mid_pad, first_off, second_off)) * scale_two).astype(
+            jnp.bfloat16
         )
+        start = pair * 192
+        if start + 192 <= 896:
+            grads[start : start + 192, 0:64] = grad_two
+        elif start >= 896:
+            grads[start - 896 : start - 704, 64:128] = grad_two
+        else:
+            grads[start:896, 0:64] = grad_two[: 896 - start]
+            grads[0 : start - 704, 64:128] = grad_two[896 - start :]
         total = total + matmul(
             window(del_pad, first_off, second_off), k_back[pair], ((1,), (1,))
         )
@@ -214,26 +273,97 @@
     delta_one = jnp.concatenate(
         [pre_one[pl.ds(slot, 128, stride=batch), :] for slot in range(batch)], axis=0
     ).astype(jnp.bfloat16)
-    grad_one_ref[...] = matmul(columns, delta_one) * scale_one
-
-
-def forward_back(rows, aims, valid, k_first, k_second, w_hidden, w_out):
-    batch = rows.shape[0]
-    k_pairs = k_second.reshape(9, 192, 64)
+    grads[832:896, 64:128] = (matmul(columns, delta_one) * scale_one).astype(jnp.bfloat16)
+    if n * per > 896:
+        grads[896 : n * per, :] = jnp.zeros((n * per - 896, 128), jnp.bfloat16)
+    scatter = []
+    for hop in range(1, n):
+        peer = lax.rem(me + hop, n)
+        chunk = grads.at[pl.ds(pl.multiple_of(peer * per, 16), per)]
+        scatter.append(remote(chunk, grads_in.at[hop], sems, 4, hop, "stream", peer))
+    for copy in scatter:
+        copy.start()
+
+    for copy in copies:
+        copy.wait_recv()
+    for hop in range(n):
+        pair = feat_in[hop].astype(jnp.float32)
+        feat_all[hop * batch : hop * batch + batch, 0:1024] = pair[:batch]
+        feat_all[hop * batch : hop * batch + batch, 1024:2048] = pair[batch:]
+    grad_out = [jnp.zeros((1, 2048), jnp.float32), jnp.zeros((1, 2048), jnp.float32)]
+    group = 64 // batch
+    for part in range(n // group):
+        span = slice(part * 64, part * 64 + 64)
+        tails = tail_in[part * group : part * group + group].reshape(64, 128)
+        _, sums, delta_part = head(dense(feat_all[span, :].astype(jnp.bfloat16)), w_out, tails)
+        delta_all[span, :] = delta_part
+        grad_out = [old + new for old, new in zip(grad_out, sums)]
+    square = (jnp.sum(grad_out[0] * grad_out[0]) + jnp.sum(grad_out[1] * grad_out[1])) / 4096.0
+    for i in range(2):
+        new_out[i : i + 1, :] = w_out[i : i + 1, :] - learn_rate * grad_out[i] * lax.rsqrt(
+            square + rms_eps
+        )
+
+    total = grads[pl.ds(pl.multiple_of(me * per, 16), per), :].astype(jnp.float32)
+    for hop in range(1, n):
+        scatter[hop - 1].wait_recv()
+        total = total + grads_in[hop].astype(jnp.float32)
+    left = jnp.mean(total[:, :64] * total[:, :64], axis=1, keepdims=True) + rms_eps
+    right = jnp.mean(total[:, 64:] * total[:, 64:], axis=1, keepdims=True) + rms_eps
+    lane_all = lax.broadcasted_iota(jnp.int32, (per, 128), 1)
+    update[me] = (total * jnp.where(lane_all < 64, lax.rsqrt(left), lax.rsqrt(right))).astype(
+        jnp.bfloat16
+    )
+    gather = []
+    for hop in range(1, n):
+        peer = lax.rem(me + hop, n)
+        gather.append(remote(update.at[me], update.at[me], sems, 6, hop, "stream", peer))
+    for copy in gather:
+        copy.start()
+
+    if share % 128 == 0:
+        own_feat = feat_all[:, pl.ds(pl.multiple_of(me * share, 128), share)]
+    else:
+        picks = lax.broadcasted_iota(jnp.int32, (2048, share), 0) - me * share
+        hot = picks == lax.broadcasted_iota(jnp.int32, (2048, share), 1)
+        own_feat = matmul(feat_all[...].astype(jnp.bfloat16), jnp.where(hot, 1.0, 0.0).astype(jnp.bfloat16))
+    own_feat = own_feat.T.astype(jnp.bfloat16)
+    for part in range(share // 64):
+        grad = matmul(own_feat[part * 64 : part * 64 + 64], delta_all[...]) * scale_dense
+        rate = learn_rate * lax.rsqrt(jnp.mean(grad * grad, axis=1, keepdims=True) + rms_eps)
+        weight = w_vmem[pl.ds(pl.multiple_of(me * share + part * 64, 64), 64), :]
+        new_hidden[part * 64 : part * 64 + 64, :] = weight.astype(jnp.float32) - grad * rate
+
+    for copy in returns:
+        copy.wait_recv()
+    back_ref[...] = pred_in[...]
+    for copy in gather:
+        copy.wait_recv()
+    step = update[...].reshape(n * per, 128).astype(jnp.float32) * learn_rate
+    new_second[0:896, :] = k_second[0:896, :].astype(jnp.float32) - step[:896, :64]
+    new_second[896:1728, :] = k_second[896:1728, :].astype(jnp.float32) - step[:832, 64:]
+    new_first[...] = k_first[...].astype(jnp.float32) - step[832:896, 64:]
+    for copy in copies + returns + scatter + gather:
+        copy.wait_send()
+
+
+def train(parcel, k_first, k_second, w_hidden, w_out):
+    batch = parcel.shape[0]
+    n, walls = lax.axis_size("stream"), lax.axis_size("wall")
+    per = -(-896 // (n * 16)) * 16
     k_back = k_second.reshape(9, 3, 64, 64).transpose(0, 2, 1, 3).reshape(9, 64, 192)
     vmem = pl.BlockSpec(memory_space=pltpu.VMEM)
     return pl.pallas_call(
-        network,
+        functools.partial(network, n, walls, per),
         out_shape=(
-            jax.ShapeDtypeStruct((batch, 2), jnp.float32),
+            jax.ShapeDtypeStruct((walls, batch, 128), jnp.float32),
             jax.ShapeDtypeStruct((64, 64), jnp.float32),
-            jax.ShapeDtypeStruct((9, 192, 64), jnp.float32),
+            jax.ShapeDtypeStruct((1728, 64), jnp.float32),
+            jax.ShapeDtypeStruct((2048 // n, 2048), jnp.float32),
             jax.ShapeDtypeStruct((2, 2048), jnp.float32),
-            jax.ShapeDtypeStruct((batch, 2048), jnp.bfloat16),
-            jax.ShapeDtypeStruct((batch, 2048), jnp.bfloat16),
         ),
-        in_specs=[vmem] * 6 + [pl.BlockSpec(memory_space=pl.ANY), vmem],
-        out_specs=(vmem,) * 6,
+        in_specs=[vmem] * 4 + [pl.BlockSpec(memory_space=pl.ANY), vmem],
+        out_specs=(vmem,) * 5,
         scratch_shapes=[
             pltpu.VMEM((2048, 2048), jnp.bfloat16),
             pltpu.VMEM((64 * batch, 128), jnp.float32),
@@ -243,30 +373,30 @@
             pltpu.VMEM((6, 6, 8 * batch, 64), jnp.bfloat16),
             pltpu.VMEM((128 * batch, 64), jnp.float32),
             pltpu.VMEM((4, 8, batch, 64), jnp.float32),
+            pltpu.VMEM((n, 2 * batch, 1024), jnp.bfloat16),
+            pltpu.VMEM((n, batch, 128), jnp.float32),
+            pltpu.VMEM((n * batch, 2048), jnp.float32),
+            pltpu.VMEM((n * batch, 2048), jnp.bfloat16),
+            pltpu.VMEM((n * per, 128), jnp.bfloat16),
+            pltpu.VMEM((n, per, 128), jnp.bfloat16),
+            pltpu.VMEM((n, per, 128), jnp.bfloat16),
+            pltpu.VMEM((walls, batch, 128), jnp.float32),
             pltpu.SemaphoreType.DMA,
+            pltpu.SemaphoreType.DMA((8, n)),
+            pltpu.SemaphoreType.DMA((2, walls)),
         ],
-        compiler_params=pltpu.CompilerParams(vmem_limit_bytes=48 * 1024 * 1024),
+        compiler_params=pltpu.CompilerParams(
+            vmem_limit_bytes=52 * 1024 * 1024, collective_id=0, has_side_effects=True
+        ),
     )(
-        rows, aims, valid, jnp.pad(k_first, ((0, 10), (0, 0))), k_pairs, k_back, w_hidden,
+        parcel, jnp.pad(k_first, ((0, 10), (0, 0))), k_second.reshape(1728, 64), k_back, w_hidden,
         w_out.T.astype(jnp.float32),
     )
-
-
-def row_update(weight, grad):
-    scale = jnp.sqrt(jnp.mean(grad * grad, axis=-1, keepdims=True) + rms_eps)
-    return weight.astype(jnp.float32) - learn_rate * grad / scale
-
-
-def whole_update(weight, grad):
-    scale = jnp.sqrt(jnp.mean(grad * grad) + rms_eps)
-    return weight.astype(jnp.float32) - learn_rate * grad / scale
 
 
 def body(velocity, sample_block, sample_member, k_first, k_second, w_hidden, w_out):
     wall_count = lax.axis_size("wall")
     wall_place = lax.axis_index("wall")
-    flow_count = lax.axis_size("stream")
-    flow_place = lax.axis_index("stream")
     padded = with_halo(velocity, (("wall", 1), ("stream", 2)), 1)
     keep_low = (wall_place > 0).astype(jnp.float32)
     keep_high = (wall_place < wall_count - 1).astype(jnp.float32)
@@ -325,33 +455,19 @@
         [send_rows, send_aims, send_valid[:, None], jnp.zeros((select.shape[0], 125), jnp.bfloat16)], axis=1
     )
     parcel = lax.all_to_all(parcel, "wall", split_axis=0, concat_axis=0, tiled=True)
-    tail = parcel[:, 256:259].astype(jnp.float32)
-    pred, grad_one, grad_two, grad_out, features, delta_three = forward_back(
-        parcel[:, :256], tail[:, 0:2], tail[:, 2:3], k_first[0], k_second[0], w_hidden[0], w_out[0]
-    )
-    grad_one = grad_one[:54]
-    grad_two = grad_two.reshape(27, 64, 64)
-    back = lax.all_to_all(pred, "wall", split_axis=0, concat_axis=0, tiled=True)
+    gathered, new_first, new_second, new_w_hidden, new_out = train(
+        parcel, k_first[0], k_second[0], w_hidden[0], w_out[0]
+    )
+    mine = lax.dynamic_slice_in_dim(gathered[:, :, :2], wall_place * CAP, CAP, 1)
+    source = (wall_place - jnp.arange(wall_count)) % wall_count
+    order = (source[None, :] == jnp.arange(wall_count)[:, None]).astype(jnp.float32)
+    back = jnp.einsum("ph,hrk->prk", order, mine, precision=highest).reshape(-1, 2)
     stress_local = jnp.dot(select.T, back, precision=highest)
     stress = stress_local.T[:, None, :]
-    share_rows = FEATS // flow_count
-    dense_scale = 1.0 / math.sqrt(1.0 * FEATS)
-    columns_here = lax.all_to_all(features, "stream", split_axis=1, concat_axis=0, tiled=True)
-    grad_hidden = (
-        jnp.dot(
-            columns_here.T,
-            lax.all_gather(delta_three, "stream", axis=0, tiled=True),
-            preferred_element_type=jnp.float32,
-        )
-        * dense_scale
-    )
-    own_rows = lax.dynamic_slice_in_dim(w_hidden[0], flow_place * share_rows, share_rows, 0)
-    new_w_hidden = row_update(own_rows, grad_hidden)[None]
-    grad_one, grad_two, grad_out = lax.psum((grad_one, grad_two, grad_out), "stream")
-    new_k_second = row_update(k_second[0], grad_two)
-    new_k_first = row_update(k_first[0], grad_one)
-    new_w_out = whole_update(w_out[0], grad_out.T)
-    return (new_field, stress, new_k_first[None], new_k_second[None], new_w_hidden, new_w_out[None])
+    return (
+        new_field, stress, new_first[None, :54], new_second.reshape(k_second.shape),
+        new_w_hidden[None], new_out.T[None],
+    )
 
 
 def solution(mesh):

time: 136 us -> 73.9 us (0.54)
  blocking collectives: 43.7 us -> 0 us
  between operations: 15.1 us -> 1.02 us
  Pallas kernels: 14.1 us -> 25.2 us
  other arithmetic: 17.3 us -> 10.6 us
  starting transfers between devices: 16.9 us -> 10.3 us
  waiting for transfers between devices: 5.22 us -> 1.44 us
  local copies, waits for them, and re-layouts: 15.1 us -> 17.5 us
    psum x1 -> x0, blocking collectives: 28.9 us -> none  [body(): lax.psum((grad_one, grad_two, grad_out), 'stream')]
    all_gather x1 -> x0, blocking collectives: 14.8 us -> none  [body(): lax.all_gather(delta_three, 'stream', axis=0, tiled=True)]
    pallas_call x1, Pallas kernels: 14.1 us -> 25.2 us  [train(): pl.pallas_call(functools.partial(network, n, walls, per), out_shape=(jax....]
    all_to_all x2 -> x0, starting transfers between devices: 6.58 us -> none  [the longest x1 3.32 us: body(): lax.all_to_all(features, 'stream', split_axis=1, concat_axis=0, tiled=True)]
    broadcast_in_dim x4 -> x0, other arithmetic: 6.13 us -> none  [the longest x1 3.03 us: body(): new_w_hidden = row_update(own_rows, grad_hidden)[None]]
    all_to_all x2 -> x0, waiting for transfers between devices: 3.76 us -> none  [the longest x1 3.75 us: body(): lax.all_to_all(features, 'stream', split_axis=1, concat_axis=0, tiled=True)]
    unnamed x34 -> x43, local copies, waits for them, and re-layouts: 2.07 us -> 4.92 us
    reduce_sum x3 -> x0, other arithmetic: 2.19 us -> none  [the longest x2 1.58 us: row_update(): scale = jnp.sqrt(jnp.mean(grad * grad, axis=-1, keepdims=True) + rms_eps)]
  transfers between devices with their start and end apart: 8 -> 5, of which waited for: 2 -> 1; matrix products, arithmetic and copies ran while one was open for 20% -> 30% of each run, Pallas kernels for 10% -> 35%
where the time goes in v2:
time: 73.9 us; the launch traced here: 72.8 us
  Pallas kernels  25.2 us (34%)
  local copies, waits for them, and re-layouts  17.5 us (24%)
  other arithmetic  10.6 us (14%)
  starting transfers between devices  10.3 us (14%)
  matrix products  6.66 us (9%)
  waiting for transfers between devices  1.44 us (2%)
  between operations  1.02 us (1%)
    pallas_call x1, Pallas kernels, train(): pl.pallas_call(functools.partial(network, n, walls, per), out_shape=(jax....  25.2 us
    ppermute x2, starting transfers between devices, with_halo(): after = lax.ppermute(first, axis, down)  6.16 us
    unnamed x43, local copies, waits for them, and re-layouts  4.92 us
    all_to_all x1, starting transfers between devices, body(): lax.all_to_all(parcel, 'wall', split_axis=0, concat_axis=0, tiled=True)  4.19 us
    slice x2, local copies, waits for them, and re-layouts, with_halo(): first = lax.slice_in_dim(shard, 0, width, axis=dim)  2.36 us
    dot_general x1, matrix products, body(): along_z = jnp.einsum('cyxz,wz->cyxw', velocity, pair_z, precision=highest)  2.22 us
    reshape x1, local copies, waits for them, and re-layouts, body(): jnp.stack([grad_y[0], grad_y[2]])  2.14 us
    add x1, other arithmetic, body(): velocity + time_step * (-advect - relax_rate * (high_x + high_y + high_z))  1.9 us
  transfers between devices with their start and end apart: 5, of which 1 were waited for; matrix products, arithmetic and copies ran while one was open for 30% of the time, Pallas kernels for 35%

profile of v2, /device:TPU:0, one launch (start us, length us, event | category | flops | bytes accessed | tf_op | source)
XLA Modules:
  0.0 72.8 jit_solution(4964666952947490099)
XLA Ops:
  0.6 1.4 %fusion.30 = (f32[3,1,16,128]{3,2,1,0:T(8,128)}, f32[3,1,16,128]{3,2,1,0:T(8,128)}) fusion(f32[3,8,16,128]{3,2,1,0:T(8,128)} %param.18), kind=kLoop, calls=%fused_computation.73 | loop fusion | bytes 98304 | tf_op jit(solution)/shard_map/slice | solution.py:39
  2.0 3.9 %collective-permute-start.1 = (f32[3,1,16,128]{3,2,1,0:T(8,128)}, f32[3,1,16,128]{3,2,1,0:T(8,128)S(1)}, u32[]{:S(2)}, u32[]{:S(2)}) collective-permute-start(f32[3,1,16,128]{3,2,1,0:T(8,128)} %get-tuple-element.97), channel_id=1, source_target_pairs={{8,0},{16,8},{24,16},{0,24},{9,1},{17,9},{25,17},{1,25},{10,2},{18... | collective-permute-start | bytes 73736 | tf_op jit(solution)/shard_map/ppermute | solution.py:41
  5.9 0.7 compare_and_fusion
  6.6 0.7 fusion.24
  7.2 0.9 %fusion.28 = (bf16[1,8,16,128]{3,2,1,0:T(8,128)(2,1)S(1)}, bf16[1,8,16,128]{3,2,1,0:T(8,128)(2,1)S(1)}) fusion(f32[3,8,16,128]{3,2,1,0:T(8,128)} %param.18), kind=kLoop, calls=%fused_computation.71 | loop fusion | bytes 131072 | tf_op jit(solution)/shard_map/slice | solution.py:432
  8.1 1.6 %slice_bitcast_fusion.3 = (f32[8,16,128]{2,1,0:T(8,128)S(1)}, f32[8,16,128]{2,1,0:T(8,128)}, f32[8,16,128]{2,1,0:T(8,128)}) fusion(f32[3,8,16,128]{3,2,1,0:T(8,128)} %param.18), kind=kLoop, calls=%fused_computation.69 | loop fusion | bytes 393216 | tf_op jit(solution)/shard_map/mul | solution.py:432
  9.7 0.7 fusion.14
  10.4 0.8 %select_reduce_fusion = s32[4]{0:T(128)S(1)} fusion(s32[4,4]{1,0:T(4,128)S(1)} %reduce_window_sum.11, s32[4]{0:T(128)} %bitcast.93), kind=kLoop, calls=%fused_computation.48 | loop fusion | flops 76 | bytes 96 | tf_op jit(solution)/shard_map/reduce_sum | solution.py:83
  11.3 0.7 multiply_add_fusion
  12.1 0.7 convert_bitcast_fusion.w_out
  12.8 1.4 %convolution_bitcast_fusion.1 = f32[3,8,32,128]{3,2,1,0:T(8,128)S(1)} fusion(f32[32,16,1,1]{0,1,3,2:T(8,128)} %constant.202, f32[3,8,16,128]{3,2,1,0:T(8,128)} %param.18), kind=kOutput, calls=%fused_computation.3 | convolution fusion | flops 18874368 | bytes 591872 | tf_op jit(solution)/shard_map/cyxz,wx->cywz/dot_general | solution.py:420
  14.2 1.6 %fusion.6 = f32[16,3,16,128]{3,0,2,1:T(8,128)S(1)} fusion(f32[16,8,1,1]{0,1,3,2:T(8,128)} %constant.203, f32[3,8,16,128]{3,2,1,0:T(8,128)} %param.18), kind=kOutput, calls=%fused_computation.16 | convolution fusion | flops 9437184 | bytes 590336 | tf_op jit(solution)/shard_map/cyxz,wy->cwxz/dot_general | solution.py:411
  15.8 2.2 %convolution_bitcast_fusion = f32[3,8,16,256]{3,2,1,0:T(8,128)} fusion(f32[256,128,1,1]{1,0,3,2:T(8,128)} %constant.204, f32[3,8,16,128]{3,2,1,0:T(8,128)} %param.18), kind=kOutput, calls=%fused_computation.2 | convolution fusion | flops 150994944 | bytes 720896 | tf_op jit(solution)/shard_map/cyxz,wz->cyxw/dot_general | solution.py:429
  18.1 1.2 %reshape.254 = bf16[2,2,4,4,4,16,8]{6,5,4,3,2,1,0:T(8,128)(2,1)S(1)} reshape(bf16[2,8,16,128]{3,2,1,0:T(8,128)(2,1)S(1)} %pad_maximum_fusion) | data formatting | bytes 131072 | tf_op jit(solution)/shard_map/reshape | solution.py:435
  23.2 0.7 %constant_dynamic-update-slice_fusion.2 = (f32[3,10,16,128]{3,2,1,0:T(8,128)S(1)}, f32[3,8,16,128]{3,2,1,0:T(8,128)S(1)}) fusion(f32[3,1,16,128]{3,2,1,0:T(8,128)} %collective-permute-done, f32[3,8,16,128]{3,2,1,0:T(8,128)S(1)} %slice.203, f32[]{:T(128)S(6)} %convert_element_type.51, f32[3,16,16,128]{3,2,1,0:T(8,128)S(1)} %bitcast.86), kind=kLoop, calls=%fused_computation.34 | loop fusion | flops 18431 | bytes 98308
  24.0 0.7 copy-done.10
  24.7 0.7 copy-done.6
  25.4 0.7 pad_maximum_fusion.1
  26.1 2.1 %reshape.257 = f32[2,2,4,4,4,16,8]{6,5,4,3,2,1,0:T(8,128)S(1)} reshape(f32[2,8,16,128]{3,2,1,0:T(8,128)} %pad_maximum_fusion.1) | data formatting | bytes 262144 | tf_op jit(solution)/shard_map/reshape | solution.py:437
  28.6 0.7 gather_fusion.1
  29.6 0.7 maximum_maximum_fusion
  30.3 4.2 %all-to-all-start = ((bf16[4,2,384]{2,1,0:T(2,128)(2,1)}), bf16[4,2,384]{2,1,0:T(2,128)(2,1)S(1)}, u32[]{:S(2)}, u32[]{:S(2)}) async-start(bf16[4,2,384]{2,1,0:T(2,128)(2,1)} %maximum_maximum_fusion), calls=%async_computation | async-start | bytes 12288 | tf_op jit(solution)/shard_map/all_to_all | solution.py:457
  34.5 1.0 %fusion.27 = (f32[3,10,1,128]{3,2,1,0:T(1,128)S(1)}, f32[3,10,1,128]{3,2,1,0:T(1,128)S(1)}) fusion(f32[3,10,16,128]{3,2,1,0:T(8,128)} %copy-done.10), kind=kLoop, calls=%fused_computation.70 | loop fusion | bytes 61440 | tf_op jit(solution)/shard_map/slice | solution.py:39
  35.5 2.3 %collective-permute-start.3 = (f32[3,10,1,128]{3,2,1,0:T(1,128)S(1)}, f32[3,10,1,128]{3,2,1,0:T(1,128)}, u32[]{:S(2)}, u32[]{:S(2)}) collective-permute-start(f32[3,10,1,128]{3,2,1,0:T(1,128)S(1)} %get-tuple-element.88), channel_id=1, source_target_pairs={{1,0},{2,1},{3,2},{4,3},{5,4},{6,5},{7,6},{0,7},{9,8},{10,9},{11,1... | collective-permute-start | bytes 46088 | tf_op jit(solution)/shard_map/ppermute | solution.py:41
  37.8 1.4 %all-to-all-done = bf16[4,2,384]{2,1,0:T(2,128)(2,1)S(1)} async-done(((bf16[4,2,384]{2,1,0:T(2,128)(2,1)}), bf16[4,2,384]{2,1,0:T(2,128)(2,1)S(1)}, u32[]{:S(2)}, u32[]{:S(2)}) %all-to-all-start) | async-done | bytes 6176 | tf_op jit(solution)/shard_map/all_to_all | solution.py:457
  39.3 25.2 %shard_map.145 = (f32[4,8,128]{2,1,0:T(8,128)S(1)}, f32[64,64]{1,0:T(8,128)S(1)}, f32[1728,64]{1,0:T(8,128)S(1)}, f32[256,2048]{1,0:T(8,128)}, f32[2,2048]{1,0:T(2,128)S(1)}) custom-call(bf16[8,384]{1,0:T(8,128)(2,1)S(1)} %all_to_all.6.parcel, bf16[64,64]{1,0:T(8,128)(2,1)S(1)} %pad.12.k_first, bf16[1728,64]{1,0:T(8,128)(2,1)S(1)} %bitcast.77, ...), custom_call_target="tpu_custom_call" | custom-call | tf_op jit(solution)/shard_map/pallas_call | solution.py:356
  64.9 0.8 %fusion.13 = f32[2,4]{1,0:T(2,128)} fusion(f32[8,2]{0,1:T(2,128)S(1)} %reshape.260, s32[4]{0:T(128)S(1)} %copy-done.16), kind=kOutput, calls=%fused_computation.47 | convolution fusion | flops 800 | bytes 112 | tf_op jit(solution)/shard_map/dot_general | solution.py:465
  66.3 0.7 %fusion.11 = f32[3,8,1,128]{3,2,1,0:T(1,128)S(1)} fusion(f32[3,10,1,128]{3,2,1,0:T(1,128)} %collective-permute-done.2, f32[3,8,32,128]{3,2,1,0:T(8,128)S(1)} %copy-done.4), kind=kLoop, calls=%fused_computation.30 | loop fusion | flops 6144 | bytes 36864 | tf_op jit(solution)/shard_map/add | solution.py:424
  67.2 0.7 %fusion.10 = f32[3,8,1,128]{3,2,1,0:T(1,128)S(1)} fusion(f32[3,10,1,128]{3,2,1,0:T(1,128)} %collective-permute-done.3, f32[3,8,16,128]{3,2,1,0:T(8,128)S(1)} %scatter-add.14), kind=kLoop, calls=%fused_computation.28 | loop fusion | flops 6144 | bytes 36864 | tf_op jit(solution)/shard_map/add | solution.py:426
  68.0 1.9 %fusion.3 = f32[3,8,16,128]{3,2,1,0:T(8,128)} fusion(f32[3,8,16,128]{3,2,1,0:T(8,128)S(1)} %copy-done.1, f32[3,8,16,256]{3,2,1,0:T(8,128)S(1)} %copy-done.5, f32[3,16,16,128]{3,2,1,0:T(8,128)S(1)} %bitcast.87, f32[3,8,32,128]{3,2,1,0:T(8,128)S(1)} %copy-done.4, f32[3,8,16,128]{3,2,1,0:T(8,128)} %copy-done.6, f32[3,8,16,128]{3,2,1,0:T(8,128)S(1)} %scatter-add.15, ...), kind=kLoop, calls=%fused_computation.11 | loop fusion | flops 589824 | bytes 1769472 | tf_op jit(solution)/shard_map/add | solution.py:433
  69.9 0.9 %copy.81 = f32[1,27,64,64]{3,2,1,0:T(8,128)} copy(f32[1,27,64,64]{3,2,1,0:T(8,128)S(1)} %bitcast.78) | data formatting | bytes 884736
  70.8 1.3 %copy.82 = f32[1,256,2048]{2,1,0:T(8,128)} copy(f32[1,256,2048]{2,1,0:T(8,128)S(1)} %bitcast.83) | data formatting | bytes 4194304
  (83 shorter events, 6.7 us)
Async XLA Ops:
  2.0 22.0 %collective-permute-start.1 = (f32[3,1,16,128]{3,2,1,0:T(8,128)}, f32[3,1,16,128]{3,2,1,0:T(8,128)S(1)}, u32[]{:S(2)}, u32[]{:S(2)}) collective-permute-start(f32[3,1,16,128]{3,2,1,0:T(8,128)} %get-tuple-element.97), channel_id=1, source_target_pairs={{8,0},{16,8},{24,16},{0,24},{9,1},{17,9},{25,17},{1,25},{10,2},{18... | collective-permute-start | bytes 73736 | tf_op jit(solution)/shard_map/ppermute | solution.py:41
  5.9 17.3 %collective-permute-start = (f32[3,1,16,128]{3,2,1,0:T(8,128)}, f32[3,1,16,128]{3,2,1,0:T(8,128)}, u32[]{:S(2)}, u32[]{:S(2)}) collective-permute-start(f32[3,1,16,128]{3,2,1,0:T(8,128)} %get-tuple-element.98), channel_id=1, source_target_pairs={{0,8},{8,16},{16,24},{24,0},{1,9},{9,17},{17,25},{25,1},{2,10},{10... | collective-permute-start | bytes 73736 | tf_op jit(solution)/shard_map/ppermute | solution.py:40
  6.6 14.4 %copy-start.17 = (pred[4]{0:T(512)(128)(4,1)}, pred[4]{0:T(512)(128)(4,1)S(1)}, u32[]{:S(2)}) copy-start(pred[4]{0:T(512)(128)(4,1)S(1)} %compare_and_fusion) | copy-start | bytes 16
  11.9 9.0 %copy-start.14 = (s32[4]{0:T(128)}, s32[4]{0:T(128)S(1)}, u32[]{:S(2)}) copy-start(s32[4]{0:T(128)S(1)} %multiply_add_fusion) | copy-start | bytes 52
  12.0 8.3 %copy-start.11 = (s32[1024]{0:T(1024)}, s32[1024]{0:T(1024)S(1)}, u32[]{:S(2)}) copy-start(s32[1024]{0:T(1024)S(1)} %pad_clamp_fusion) | copy-start | bytes 12292
  14.2 7.7 %copy-start.3 = (f32[3,8,32,128]{3,2,1,0:T(8,128)}, f32[3,8,32,128]{3,2,1,0:T(8,128)S(1)}, u32[]{:S(2)}) copy-start(f32[3,8,32,128]{3,2,1,0:T(8,128)S(1)} %convolution_bitcast_fusion.1) | copy-start | bytes 1179652
  19.3 2.8 %copy-start = (bf16[1,27,64,64]{3,2,1,0:T(8,128)(2,1)S(1)}, bf16[1,27,64,64]{3,2,1,0:T(8,128)(2,1)}, u32[]{:S(2)}) copy-start(bf16[1,27,64,64]{3,2,1,0:T(8,128)(2,1)} %param.22) | copy-start | bytes 663556
  19.9 2.7 %copy-start.9 = (bf16[1,54,64]{2,1,0:T(8,128)(2,1)S(1)}, bf16[1,54,64]{2,1,0:T(8,128)(2,1)}, u32[]{:S(2)}) copy-start(bf16[1,54,64]{2,1,0:T(8,128)(2,1)} %param.21) | copy-start | bytes 20740
  19.9 4.1 %copy-start.1 = (f32[3,8,16,128]{3,2,1,0:T(8,128)S(1)}, f32[3,8,16,128]{3,2,1,0:T(8,128)}, u32[]{:S(2)}) copy-start(f32[3,8,16,128]{3,2,1,0:T(8,128)} %param.18) | copy-start | bytes 589828
  24.0 0.7 copy-start.10
  24.7 0.7 copy-start.6
  26.0 3.2 %copy-start.15 = (s32[4]{0:T(128)S(1)}, s32[4]{0:T(128)}, u32[]{:S(2)}) copy-start(s32[4]{0:T(128)} %copy-done.14) | copy-start | bytes 52
  26.1 3.2 %copy-start.18 = (pred[4]{0:T(512)(128)(4,1)S(1)}, pred[4]{0:T(512)(128)(4,1)}, u32[]{:S(2)}) copy-start(pred[4]{0:T(512)(128)(4,1)} %copy-done.17) | copy-start | bytes 16
  26.1 3.6 %copy-start.12 = (bf16[384]{0:T(512)(128)(2,1)S(1)}, bf16[384]{0:T(512)(128)(2,1)}, u32[]{:S(2)}) copy-start(bf16[384]{0:T(512)(128)(2,1)} %pad.16.clone) | copy-start | bytes 2308
  30.3 8.9 %all-to-all-start = ((bf16[4,2,384]{2,1,0:T(2,128)(2,1)}), bf16[4,2,384]{2,1,0:T(2,128)(2,1)S(1)}, u32[]{:S(2)}, u32[]{:S(2)}) async-start(bf16[4,2,384]{2,1,0:T(2,128)(2,1)} %maximum_maximum_fusion), calls=%async_computation | async-start | bytes 12288 | tf_op jit(solution)/shard_map/all_to_all | solution.py:457
  35.5 31.7 %collective-permute-start.3 = (f32[3,10,1,128]{3,2,1,0:T(1,128)S(1)}, f32[3,10,1,128]{3,2,1,0:T(1,128)}, u32[]{:S(2)}, u32[]{:S(2)}) collective-permute-start(f32[3,10,1,128]{3,2,1,0:T(1,128)S(1)} %get-tuple-element.88), channel_id=1, source_target_pairs={{1,0},{2,1},{3,2},{4,3},{5,4},{6,5},{7,6},{0,7},{9,8},{10,9},{11,1... | collective-permute-start | bytes 46088 | tf_op jit(solution)/shard_map/ppermute | solution.py:41
  37.8 28.6 %collective-permute-start.2 = (f32[3,10,1,128]{3,2,1,0:T(1,128)S(1)}, f32[3,10,1,128]{3,2,1,0:T(1,128)}, u32[]{:S(2)}, u32[]{:S(2)}) collective-permute-start(f32[3,10,1,128]{3,2,1,0:T(1,128)S(1)} %get-tuple-element.89), channel_id=1, source_target_pairs={{0,1},{1,2},{2,3},{3,4},{4,5},{5,6},{6,7},{7,0},{8,9},{9,10},{10,1... | collective-permute-start | bytes 46088 | tf_op jit(solution)/shard_map/ppermute | solution.py:40
  39.2 25.4 %copy-start.13 = (s32[4]{0:T(128)S(1)}, s32[4]{0:T(128)}, u32[]{:S(2)}) copy-start(s32[4]{0:T(128)} %and_select_fusion) | copy-start | bytes 52
  39.2 25.7 %copy-start.16 = (s32[4]{0:T(128)S(1)}, s32[4]{0:T(128)}, u32[]{:S(2)}) copy-start(s32[4]{0:T(128)} %copy-done.14) | copy-start | bytes 52
  39.2 27.1 %copy-start.4 = (f32[3,8,32,128]{3,2,1,0:T(8,128)S(1)}, f32[3,8,32,128]{3,2,1,0:T(8,128)}, u32[]{:S(2)}) copy-start(f32[3,8,32,128]{3,2,1,0:T(8,128)} %copy-done.3) | copy-start | bytes 1179652
  39.2 27.8 %slice-start = ((f32[3,8,32,128]{3,2,1,0:T(8,128)}), f32[3,8,16,128]{3,2,1,0:T(8,128)S(1)}, s32[]{:S(2)}) async-start(f32[3,8,32,128]{3,2,1,0:T(8,128)} %copy-done.3), calls=%async_computation.1 | async-start | bytes 393216 | tf_op jit(solution)/shard_map/slice | solution.py:422
  39.2 28.8 %copy-start.5 = (f32[3,8,16,256]{3,2,1,0:T(8,128)S(1)}, f32[3,8,16,256]{3,2,1,0:T(8,128)}, u32[]{:S(2)}) copy-start(f32[3,8,16,256]{3,2,1,0:T(8,128)} %convolution_bitcast_fusion) | copy-start | bytes 1179652
  39.2 28.8 %copy-start.7 = (f32[8,16,128]{2,1,0:T(8,128)S(1)}, f32[8,16,128]{2,1,0:T(8,128)}, u32[]{:S(2)}) copy-start(f32[8,16,128]{2,1,0:T(8,128)} %get-tuple-element.95) | copy-start | bytes 196612
  39.3 28.8 %copy-start.8 = (f32[8,16,128]{2,1,0:T(8,128)S(1)}, f32[8,16,128]{2,1,0:T(8,128)}, u32[]{:S(2)}) copy-start(f32[8,16,128]{2,1,0:T(8,128)} %get-tuple-element.96) | copy-start | bytes 196612
  68.0 2.9 %copy-start.2 = (f32[256,2048]{1,0:T(8,128)S(1)}, f32[256,2048]{1,0:T(8,128)}, u32[]{:S(2)}) copy-start(f32[256,2048]{1,0:T(8,128)} %get-tuple-element.62) | copy-start | bytes 6291460

commit v3 on v2

--- a/solution.py
+++ b/solution.py
@@ -10,9 +10,6 @@
 from jax.sharding import PartitionSpec as P
 
 P_SIZE = 8
-PY = 4
-PX = 4
-PZ = 8
 CAP = 2
 
 
@@ -30,19 +27,6 @@
 ]
 
 
-def with_halo(shard, sides, width):
-    for axis, dim in sides:
-        size, length = (lax.axis_size(axis), shard.shape[dim])
-        up = [(i, (i + 1) % size) for i in range(size)]
-        down = [(j, i) for i, j in up]
-        last = lax.slice_in_dim(shard, length - width, length, axis=dim)
-        first = lax.slice_in_dim(shard, 0, width, axis=dim)
-        before = lax.ppermute(last, axis, up)
-        after = lax.ppermute(first, axis, down)
-        shard = jnp.concatenate([before, shard, after], axis=dim)
-    return shard
-
-
 def cheb_tables(points):
     order = points - 1
     node_index = np.arange(points)
@@ -57,34 +41,21 @@
     return (deriv, highpass, 0.5 * order * order)
 
 
-def axis_matrices(count, periodic):
-    deriv, highpass, lift_half = cheb_tables(P_SIZE)
-    length = count * P_SIZE
-    slope = np.kron(np.eye(count), deriv)
-    upper = np.kron(np.eye(count), highpass)
-    faces = count if periodic else count - 1
-    for element in range(faces):
+def element_tables():
+    slope, upper, lift = cheb_tables(P_SIZE)
+    slope[0, 0] += lift
+    slope[7, 7] -= lift
+    return slope, upper, lift
+
+
+def axis_matrix(count, slope, lift):
+    whole = np.kron(np.eye(count), slope)
+    for element in range(count):
         last_node = element * P_SIZE + P_SIZE - 1
         next_node = (element + 1) % count * P_SIZE
-        slope[last_node, next_node] += lift_half
-        slope[last_node, last_node] -= lift_half
-        slope[next_node, last_node] -= lift_half
-        slope[next_node, next_node] += lift_half
-    if not periodic:
-        slope[0, 0] += lift_half
-        slope[length - 1, length - 1] -= lift_half
-    paired = jnp.asarray(np.concatenate([slope, upper], axis=0), jnp.float32)
-    return (paired, lift_half)
-
-
-def slot_matrix(members, member_count):
-    member_hot = (members[..., None] == jnp.arange(member_count, dtype=jnp.int32)).astype(jnp.int32)
-    before = jnp.cumsum(member_hot, axis=-2) - member_hot
-    ranks = jnp.sum(before * member_hot, axis=-1)
-    slots = members * CAP + ranks
-    return (slots[..., None, :] == jnp.arange(member_count * CAP, dtype=jnp.int32)[:, None]).astype(
-        jnp.float32
-    )
+        whole[last_node, next_node] += lift
+        whole[next_node, last_node] -= lift
+    return whole
 
 
 def sigmoid(value):
@@ -146,11 +117,12 @@
 
 
 def network(
-    n, walls, per, parcel, k_first, k_second, k_back, w_hbm, w_out,
-    back_ref, new_first, new_second, new_hidden, new_out,
-    w_vmem, cols, pre_one, hid_pad, del_pad, mid_pad, pre_two, pooled,
+    n, walls, per, blocks, members, field, tab_x, tab_z, k_first, k_second, k_back, w_hbm, w_out,
+    new_field, stress, new_first, new_second, new_hidden, new_out,
+    patch_out, tail_out, w_vmem, cols, pre_one, hid_pad, del_pad, mid_pad, pre_two, pooled,
     feat_in, tail_in, feat_all, delta_all, grads, grads_in, update, pred_in,
-    w_sem, sems, wall_sems,
+    patch_in, tail_wall, rows_all, tails_all, face_y, face_x, edge_x,
+    w_sem, sems, wall_sems, face_sems,
 ):
     me, wall = lax.axis_index("stream"), lax.axis_index("wall")
     barrier = pltpu.get_barrier_semaphore()
@@ -164,13 +136,13 @@
             barrier, inc=1, device_id={"wall": lax.rem(wall + hop, walls)},
             device_id_type=pl.DeviceIdType.MESH,
         )
-    batch = parcel.shape[0]
+    batch = 2 * walls
     points = 128 * batch
     share = 2048 // n
-    tail = parcel[:, 256:384].astype(jnp.float32)
-    rows = parcel[:, 0:256].astype(jnp.float32)
+    samples = blocks.shape[1]
     fetch = pltpu.make_async_copy(w_hbm, w_vmem, w_sem)
     fetch.start()
+    slope, upper, lift = element_tables()
     scale_one = 1.0 / math.sqrt(54.0)
     scale_two = 1.0 / math.sqrt(1728.0)
     scale_dense = 1.0 / math.sqrt(2048.0)
@@ -180,7 +152,104 @@
     lane = lax.broadcasted_iota(jnp.int32, (batch, 128), 1)
     at = (lane // 32, (lane // 8) % 4, lane % 8)
     cols[54 * batch : 64 * batch, :] = jnp.zeros((10 * batch, 128), jnp.float32)
-    channel = [rows[:, 0:128], rows[:, 128:256]]
+    names = [members[0, k] for k in range(samples)]
+    picks = [blocks[0, k] for k in range(samples)]
+    ranks = []
+    for k in range(samples):
+        rank = jnp.int32(0)
+        for j in range(k):
+            rank = rank + jnp.where(names[j] == names[k], 1, 0)
+        ranks.append(rank)
+    hops = [lax.rem(name + walls - wall, walls) for name in names]
+
+    def by_slot(shape):
+        slot = lax.broadcasted_iota(jnp.int32, shape, 0) % batch
+        found = jnp.full(shape, -1, jnp.int32)
+        for k in range(samples):
+            found = jnp.where(slot == hops[k] * 2 + ranks[k], picks[k], found)
+        return found
+
+    wide = (16 * batch, 128)
+    found = by_slot(wide)
+    point = lax.broadcasted_iota(jnp.int32, wide, 0) // batch
+    lane_w = lax.broadcasted_iota(jnp.int32, wide, 1)
+    row_at = ((found >> 6) * 4 + point // 4) * 16 + ((found >> 4) & 3) * 4 + point % 4
+    row_hot = jnp.where((found >= 0) & (lane_w == row_at), 1.0, 0.0).astype(jnp.bfloat16)
+    fold = jnp.where(
+        lax.broadcasted_iota(jnp.int32, (128, 128), 0) % 8
+        == lax.broadcasted_iota(jnp.int32, (128, 128), 1) % 8, 1.0, 0.0
+    ).astype(jnp.bfloat16)
+    for c in range(2):
+        near = matmul(row_hot, field[2 * c].reshape(128, 128).astype(jnp.bfloat16))
+        near = jnp.where(lane_w // 8 == (found & 15), near, 0.0).astype(jnp.bfloat16)
+        folded = jnp.where(lane_w // 8 == point, matmul(near, fold), 0.0)
+        folded = jnp.sum(folded.reshape(16, batch, 128), axis=0)
+        rows_all[:, c * 128 : c * 128 + 128] = folded
+    for hop in range(walls):
+        patch_out[hop] = jnp.zeros((8, 256), jnp.float32)
+        patch_out[hop, 0:2, :] = rows_all[2 * hop : 2 * hop + 2, :]
+    edge_x[0] = field[:, :, 15, :]
+    edge_x[1] = field[:, :, 0, :]
+    pl.semaphore_wait(barrier, n + walls - 2)
+    patches = []
+    for hop in range(1, walls):
+        peer = lax.rem(wall + hop, walls)
+        patches.append(
+            remote(patch_out.at[hop], patch_in.at[hop], wall_sems, 2, hop, "wall", peer)
+        )
+    above, below = lax.rem(wall + 1, walls), lax.rem(wall + walls - 1, walls)
+    ahead, behind = lax.rem(me + 1, n), lax.rem(me + n - 1, n)
+    faces_y = [
+        remote(field.at[:, 7], face_y.at[0], face_sems, 0, 0, "wall", above),
+        remote(field.at[:, 0], face_y.at[1], face_sems, 0, 1, "wall", below),
+    ]
+    faces_x = [
+        remote(edge_x.at[0], face_x.at[0], face_sems, 2, 0, "stream", ahead),
+        remote(edge_x.at[1], face_x.at[1], face_sems, 2, 1, "stream", behind),
+    ]
+    for copy in patches + faces_y + faces_x:
+        copy.start()
+
+    for copy in faces_y:
+        copy.wait_recv()
+    keep_low = jnp.where(wall > 0, lift, 0.0)
+    keep_high = jnp.where(wall < walls - 1, lift, 0.0)
+    found = by_slot((batch, 128))
+    tail = jnp.where(lane == 2, jnp.where(found >= 0, 1.0, 0.0), 0.0)
+    for i in range(2):
+        halves = []
+        for half in range(2):
+            total = -keep_low * face_y[0, 2 * i] if half == 0 else keep_high * face_y[1, 2 * i]
+            for j in range(8):
+                weight = float(sum(slope[half * 4 : half * 4 + 4, j]))
+                total = total + weight * field[2 * i, j]
+            halves.append(total)
+        mean = jnp.zeros((batch, 128), jnp.float32)
+        for row in range(8):
+            strip = halves[row // 4][row % 4 * 4 : row % 4 * 4 + 4, :]
+            strip = jnp.sum(strip, axis=0, keepdims=True)
+            mean = mean + jnp.where((found >> 4) == row, strip, 0.0)
+        mean = jnp.where(lane // 8 == (found & 15), mean, 0.0)
+        aim = jnp.sum(mean, axis=1, keepdims=True) * (viscosity / 128.0)
+        tail = jnp.where((lane == i) & (found >= 0), aim.astype(jnp.bfloat16).astype(jnp.float32), tail)
+    tails_all[...] = tail
+    for hop in range(walls):
+        tail_out[hop] = jnp.zeros((8, 128), jnp.float32)
+        tail_out[hop, 0:2, :] = tails_all[2 * hop : 2 * hop + 2, :]
+    targets = []
+    for hop in range(1, walls):
+        peer = lax.rem(wall + hop, walls)
+        targets.append(
+            remote(tail_out.at[hop], tail_wall.at[hop], wall_sems, 4, hop, "wall", peer)
+        )
+    for copy in targets:
+        copy.start()
+
+    for copy in patches:
+        copy.wait_recv()
+    for hop in range(1, walls):
+        rows_all[2 * hop : 2 * hop + 2, :] = patch_in[hop, 0:2, :]
+    channel = [rows_all[:, 0:128], rows_all[:, 128:256]]
     for tap, offset in enumerate(tap_offsets):
         inside = None
         for place, step, size in zip(at, offset, (4, 4, 8)):
@@ -216,9 +285,13 @@
     feat_in[0] = jnp.concatenate([features[:, :1024], features[:, 1024:]], axis=0).astype(
         jnp.bfloat16
     )
+    for copy in targets:
+        copy.wait_recv()
+    for hop in range(1, walls):
+        tails_all[2 * hop : 2 * hop + 2, :] = tail_wall[hop, 0:2, :]
+    tail = tails_all[...]
     tail_in[0] = tail
     features = features.astype(jnp.bfloat16)
-    pl.semaphore_wait(barrier, n + walls - 2)
     copies = []
     for hop in range(1, n):
         peer = lax.rem(me + hop, n)
@@ -284,6 +357,42 @@
     for copy in scatter:
         copy.start()
 
+    for copy in faces_x:
+        copy.wait_recv()
+    flow = field[...]
+    split = flow.reshape(3, 8, 2, 8, 128)
+    grad_x = jnp.zeros((3, 8, 2, 8, 128), jnp.float32)
+    high = jnp.zeros((3, 8, 2, 8, 128), jnp.float32)
+    for j in range(8):
+        spread_j = split[:, :, :, j : j + 1, :]
+        grad_x = grad_x + tab_x[0, j] * spread_j
+        high = high + tab_x[1, j] * spread_j
+    left_side = jnp.concatenate([face_x[0][:, :, None], split[:, :, 0:1, 7]], axis=2)[:, :, :, None]
+    right_side = jnp.concatenate([split[:, :, 1:2, 0], face_x[1][:, :, None]], axis=2)[:, :, :, None]
+    node = lax.broadcasted_iota(jnp.int32, (1, 1, 1, 8, 128), 3)
+    grad_x = grad_x - jnp.where(node == 0, lift * left_side, 0.0)
+    grad_x = grad_x + jnp.where(node == 7, lift * right_side, 0.0)
+    grad_x = grad_x.reshape(3, 8, 16, 128)
+    high = high.reshape(3, 8, 16, 128)
+    along = lax.dot_general(
+        flow.reshape(384, 128), tab_z[...], (((1,), (0,)), ((), ())),
+        precision=highest, preferred_element_type=jnp.float32,
+    )
+    grad_z = along[:, :128].reshape(3, 8, 16, 128)
+    high = high + along[:, 128:].reshape(3, 8, 16, 128)
+    for i in range(8):
+        grad_y = float(slope[i, 0]) * flow[:, 0]
+        high_i = high[:, i] + float(upper[i, 0]) * flow[:, 0]
+        for j in range(1, 8):
+            grad_y = grad_y + float(slope[i, j]) * flow[:, j]
+            high_i = high_i + float(upper[i, j]) * flow[:, j]
+        if i == 0:
+            grad_y = grad_y - keep_low * face_y[0]
+        if i == 7:
+            grad_y = grad_y + keep_high * face_y[1]
+        advect = flow[0:1, i] * grad_x[:, i] + flow[1:2, i] * grad_y + flow[2:3, i] * grad_z[:, i]
+        new_field[:, i] = flow[:, i] + time_step * (-advect - relax_rate * high_i)
+
     for copy in copies:
         copy.wait_recv()
     for hop in range(n):
@@ -336,35 +445,49 @@
 
     for copy in returns:
         copy.wait_recv()
-    back_ref[...] = pred_in[...]
+    row_out = lax.broadcasted_iota(jnp.int32, (batch, 128), 0)
+    for k in range(samples):
+        line = jnp.zeros((batch, 128), jnp.float32)
+        for hop in range(walls):
+            away = (walls - hop) % walls
+            spot = jnp.where(hops[k] == away, 2 * away + ranks[k], -1)
+            line = line + jnp.where(row_out == spot, pred_in[hop], 0.0)
+        stress[k : k + 1, :] = jnp.sum(line, axis=0, keepdims=True)
     for copy in gather:
         copy.wait_recv()
     step = update[...].reshape(n * per, 128).astype(jnp.float32) * learn_rate
     new_second[0:896, :] = k_second[0:896, :].astype(jnp.float32) - step[:896, :64]
     new_second[896:1728, :] = k_second[896:1728, :].astype(jnp.float32) - step[:832, 64:]
-    new_first[...] = k_first[...].astype(jnp.float32) - step[832:896, 64:]
-    for copy in copies + returns + scatter + gather:
+    new_first[...] = k_first[0:54, :].astype(jnp.float32) - step[832:886, 64:]
+    for copy in copies + returns + scatter + gather + patches + targets + faces_y + faces_x:
         copy.wait_send()
 
 
-def train(parcel, k_first, k_second, w_hidden, w_out):
-    batch = parcel.shape[0]
+def train(blocks, members, field, k_first, k_second, w_hidden, w_out):
     n, walls = lax.axis_size("stream"), lax.axis_size("wall")
+    batch = CAP * walls
+    slope, upper, lift = element_tables()
+    tab_x = np.stack([slope.T, upper.T])[:, :, :, None] * np.ones((1, 1, 1, 128))
+    tab_z = np.concatenate([axis_matrix(16, slope, lift).T, np.kron(np.eye(16), upper).T], axis=1)
+    smem = pl.BlockSpec(memory_space=pltpu.SMEM)
     per = -(-896 // (n * 16)) * 16
     k_back = k_second.reshape(9, 3, 64, 64).transpose(0, 2, 1, 3).reshape(9, 64, 192)
     vmem = pl.BlockSpec(memory_space=pltpu.VMEM)
     return pl.pallas_call(
         functools.partial(network, n, walls, per),
         out_shape=(
-            jax.ShapeDtypeStruct((walls, batch, 128), jnp.float32),
-            jax.ShapeDtypeStruct((64, 64), jnp.float32),
+            jax.ShapeDtypeStruct(field.shape, jnp.float32),
+            jax.ShapeDtypeStruct((8, 128), jnp.float32),
+            jax.ShapeDtypeStruct((54, 64), jnp.float32),
             jax.ShapeDtypeStruct((1728, 64), jnp.float32),
             jax.ShapeDtypeStruct((2048 // n, 2048), jnp.float32),
             jax.ShapeDtypeStruct((2, 2048), jnp.float32),
         ),
-        in_specs=[vmem] * 4 + [pl.BlockSpec(memory_space=pl.ANY), vmem],
-        out_specs=(vmem,) * 5,
+        in_specs=[smem] * 2 + [vmem] * 6 + [pl.BlockSpec(memory_space=pl.ANY), vmem],
+        out_specs=(vmem,) * 6,
         scratch_shapes=[
+            pltpu.VMEM((walls, 8, 256), jnp.float32),
+            pltpu.VMEM((walls, 8, 128), jnp.float32),
             pltpu.VMEM((2048, 2048), jnp.bfloat16),
             pltpu.VMEM((64 * batch, 128), jnp.float32),
             pltpu.VMEM((128 * batch, 64), jnp.float32),
@@ -381,92 +504,36 @@
             pltpu.VMEM((n, per, 128), jnp.bfloat16),
             pltpu.VMEM((n, per, 128), jnp.bfloat16),
             pltpu.VMEM((walls, batch, 128), jnp.float32),
+            pltpu.VMEM((walls, 8, 256), jnp.float32),
+            pltpu.VMEM((walls, 8, 128), jnp.float32),
+            pltpu.VMEM((batch, 256), jnp.float32),
+            pltpu.VMEM((batch, 128), jnp.float32),
+            pltpu.VMEM((2, 3, 16, 128), jnp.float32),
+            pltpu.VMEM((2, 3, 8, 128), jnp.float32),
+            pltpu.VMEM((2, 3, 8, 128), jnp.float32),
             pltpu.SemaphoreType.DMA,
             pltpu.SemaphoreType.DMA((8, n)),
-            pltpu.SemaphoreType.DMA((2, walls)),
+            pltpu.SemaphoreType.DMA((6, walls)),
+            pltpu.SemaphoreType.DMA((4, 2)),
         ],
         compiler_params=pltpu.CompilerParams(
             vmem_limit_bytes=52 * 1024 * 1024, collective_id=0, has_side_effects=True
         ),
     )(
-        parcel, jnp.pad(k_first, ((0, 10), (0, 0))), k_second.reshape(1728, 64), k_back, w_hidden,
+        blocks, members, field, jnp.asarray(tab_x, jnp.float32), jnp.asarray(tab_z, jnp.float32),
+        jnp.pad(k_first, ((0, 10), (0, 0))), k_second.reshape(1728, 64), k_back, w_hidden,
         w_out.T.astype(jnp.float32),
     )
 
 
 def body(velocity, sample_block, sample_member, k_first, k_second, w_hidden, w_out):
-    wall_count = lax.axis_size("wall")
-    wall_place = lax.axis_index("wall")
-    padded = with_halo(velocity, (("wall", 1), ("stream", 2)), 1)
-    keep_low = (wall_place > 0).astype(jnp.float32)
-    keep_high = (wall_place < wall_count - 1).astype(jnp.float32)
-    below = padded[:, 0, 1:-1, :] * keep_low
-    above = padded[:, -1, 1:-1, :] * keep_high
-    left_face = padded[:, 1:-1, 0, :]
-    right_face = padded[:, 1:-1, -1, :]
-    size_y, size_x, size_z = (velocity.shape[1], velocity.shape[2], velocity.shape[3])
-    pair_y, lift_half = axis_matrices(size_y // P_SIZE, False)
-    pair_x, lift_same = axis_matrices(size_x // P_SIZE, False)
-    pair_z, lift_again = axis_matrices(size_z // P_SIZE, True)
-    along_y = jnp.einsum("cyxz,wy->cwxz", velocity, pair_y, precision=highest)
-    grad_y = (
-        along_y[:, :size_y]
-        .at[:, 0]
-        .add(-lift_half * below)
-        .at[:, size_y - 1]
-        .add(lift_half * above)
-    )
-    high_y = along_y[:, size_y:]
-    along_x = jnp.einsum("cyxz,wx->cywz", velocity, pair_x, precision=highest)
-    grad_x = (
-        along_x[:, :, :size_x]
-        .at[:, :, 0]
-        .add(-lift_half * left_face)
-        .at[:, :, size_x - 1]
-        .add(lift_half * right_face)
-    )
-    high_x = along_x[:, :, size_x:]
-    along_z = jnp.einsum("cyxz,wz->cyxw", velocity, pair_z, precision=highest)
-    grad_z = along_z[..., :size_z]
-    high_z = along_z[..., size_z:]
-    advect = velocity[0][None] * grad_x + velocity[1][None] * grad_y + velocity[2][None] * grad_z
-    new_field = velocity + time_step * (-advect - relax_rate * (high_x + high_y + high_z))
-    rows_y, rows_x, rows_z = (size_y // PY, size_x // PX, size_z // PZ)
-    tangent = jnp.stack([velocity[0], velocity[2]]).reshape(2, rows_y, PY, rows_x, PX, rows_z, PZ)
-    blocks = tangent.transpose(1, 3, 5, 0, 2, 4, 6).reshape(-1, 2 * PY * PX * PZ)
-    slope_wall = jnp.stack([grad_y[0], grad_y[2]]).reshape(2, rows_y, PY, rows_x, PX, rows_z, PZ)
-    stress_true = (
-        (viscosity * jnp.mean(slope_wall, axis=(2, 4, 6))).transpose(1, 2, 3, 0).reshape(-1, 2)
-    )
-    picked = sample_block.reshape(-1)
-    members = sample_member.reshape(-1)
-    patch_rows = jnp.take(blocks, picked, axis=0).astype(jnp.bfloat16)
-    aim_rows = jnp.take(stress_true, picked, axis=0).astype(jnp.bfloat16)
-    select = slot_matrix(members, wall_count)
-    select_half = select.astype(jnp.bfloat16)
-    send_rows = jnp.dot(select_half, patch_rows, preferred_element_type=jnp.float32).astype(
-        jnp.bfloat16
-    )
-    send_aims = jnp.dot(select_half, aim_rows, preferred_element_type=jnp.float32).astype(
-        jnp.bfloat16
-    )
-    send_valid = jnp.sum(select, axis=1).astype(jnp.bfloat16)
-    parcel = jnp.concatenate(
-        [send_rows, send_aims, send_valid[:, None], jnp.zeros((select.shape[0], 125), jnp.bfloat16)], axis=1
-    )
-    parcel = lax.all_to_all(parcel, "wall", split_axis=0, concat_axis=0, tiled=True)
-    gathered, new_first, new_second, new_w_hidden, new_out = train(
-        parcel, k_first[0], k_second[0], w_hidden[0], w_out[0]
-    )
-    mine = lax.dynamic_slice_in_dim(gathered[:, :, :2], wall_place * CAP, CAP, 1)
-    source = (wall_place - jnp.arange(wall_count)) % wall_count
-    order = (source[None, :] == jnp.arange(wall_count)[:, None]).astype(jnp.float32)
-    back = jnp.einsum("ph,hrk->prk", order, mine, precision=highest).reshape(-1, 2)
-    stress_local = jnp.dot(select.T, back, precision=highest)
-    stress = stress_local.T[:, None, :]
+    samples = sample_block.shape[1]
+    new_field, stress, new_first, new_second, new_w_hidden, new_out = train(
+        sample_block, sample_member[:, :, 0], velocity, k_first[0], k_second[0], w_hidden[0], w_out[0]
+    )
     return (
-        new_field, stress, new_first[None, :54], new_second.reshape(k_second.shape),
-        new_w_hidden[None], new_out.T[None],
+        new_field, stress[:samples, :2].T[:, None, :], new_first[None],
+        new_second.reshape(k_second.shape), new_w_hidden[None], new_out.T[None],
     )
 
 

time: 73.9 us -> 49.6 us (0.67)
  starting transfers between devices: 10.3 us -> 0 us
  other arithmetic: 10.6 us -> 0.7 us
  Pallas kernels: 25.2 us -> 34.5 us
  matrix products: 6.66 us -> 0 us
  local copies, waits for them, and re-layouts: 17.5 us -> 13.3 us
  waiting for transfers between devices: 1.44 us -> 0 us
    pallas_call x1, Pallas kernels: 25.2 us -> 34.5 us  [train(): pl.pallas_call(functools.partial(network, n, walls, per), out_shape=(jax....]
    dot_general x6 -> x0, matrix products: 6.54 us -> none  [the longest x1 2.22 us: body(): along_z = jnp.einsum('cyxz,wz->cyxw', velocity, pair_z, precision=highest)]
    ppermute x4 -> x0, starting transfers between devices: 6.16 us -> none  [the longest x2 6.16 us: with_halo(): after = lax.ppermute(first, axis, down)]
    unnamed x43 -> x20, local copies, waits for them, and re-layouts: 4.92 us -> 11 us
    all_to_all x1 -> x0, starting transfers between devices: 4.19 us -> none  [body(): lax.all_to_all(parcel, 'wall', split_axis=0, concat_axis=0, tiled=True)]
    add x4 -> x0, other arithmetic: 4.02 us -> none  [the longest x1 1.9 us: body(): velocity + time_step * (-advect - relax_rate * (high_x + high_y + high_z))]
    reshape x5 -> x0, local copies, waits for them, and re-layouts: 3.85 us -> none  [the longest x1 2.14 us: body(): jnp.stack([grad_y[0], grad_y[2]])]
    slice x7 -> x0, local copies, waits for them, and re-layouts: 3.27 us -> none  [the longest x2 2.36 us: with_halo(): first = lax.slice_in_dim(shard, 0, width, axis=dim)]
  transfers between devices with their start and end apart: 5 -> 0, of which waited for: 1 -> 0; matrix products, arithmetic and copies ran while one was open for 30% -> 0% of each run, Pallas kernels for 35% -> 0%
where the time goes in v3:
time: 49.6 us; the launch traced here: 49.1 us
  Pallas kernels  34.5 us (70%)
  local copies, waits for them, and re-layouts  13.3 us (27%)
  other arithmetic  0.7 us (1%)
  between operations  0.68 us (1%)
    pallas_call x1, Pallas kernels, train(): pl.pallas_call(functools.partial(network, n, walls, per), out_shape=(jax....  34.5 us
    unnamed x20, local copies, waits for them, and re-layouts  11 us
    another operation x1, local copies, waits for them, and re-layouts, train(): k_second.reshape(9, 3, 64, 64).transpose(0, 2, 1, 3).reshape(9, 64, 192)  1.25 us

profile of v3, /device:TPU:0, one launch (start us, length us, event | category | flops | bytes accessed | tf_op | source)
XLA Modules:
  0.0 49.1 jit_solution(15218178750568404942)
XLA Ops:
  0.6 0.7 %pad.4.k_first = bf16[64,64]{1,0:T(8,128)(2,1)S(1)} pad(bf16[54,64]{1,0:T(8,128)(2,1)} %bitcast.32, bf16[]{:T(256)} %constant.6.clone.1), padding=0_10x0_0 | pad | bytes 15106 | tf_op jit(solution)/shard_map/jit(_pad)/pad | solution.py:524
  1.4 0.7 %convert_bitcast_fusion.w_out = f32[2,2048]{1,0:T(2,128)S(1)} fusion(bf16[1,2048,2]{1,2,0:T(2,128)(2,1)} %param.15), kind=kLoop, calls=%fused_computation | loop fusion | flops 4096 | bytes 24576 | tf_op jit(solution)/shard_map/convert_element_type | solution.py:525
  2.1 1.3 %copy.19 = bf16[9,3,64,64]{2,3,1,0:T(8,128)(2,1)S(1)} copy(bf16[9,3,64,64]{3,2,1,0:T(8,128)(2,1)} %bitcast.23) | data formatting | bytes 442368 | tf_op jit(solution)/shard_map/reshape;squeeze | solution.py:474
  3.3 0.2 copy.20.k_back
  3.5 0.0 copy-start
  3.6 1.0 %copy-done = bf16[1,27,64,64]{3,2,1,0:T(8,128)(2,1)S(1)} copy-done((bf16[1,27,64,64]{3,2,1,0:T(8,128)(2,1)S(1)}, bf16[1,27,64,64]{3,2,1,0:T(8,128)(2,1)}, u32[]{:S(2)}) %copy-start) | copy-done | bytes 221208
  4.6 0.0 copy-start.1
  4.6 0.9 %copy-done.1 = f32[3,8,16,128]{3,2,1,0:T(8,128)S(1)} copy-done((f32[3,8,16,128]{3,2,1,0:T(8,128)S(1)}, f32[3,8,16,128]{3,2,1,0:T(8,128)}, u32[]{:S(2)}) %copy-start.1) | copy-done | bytes 196632
  5.5 0.0 copy-start.2
  5.5 0.9 %copy-done.2 = f32[128,256]{1,0:T(8,128)S(1)} copy-done((f32[128,256]{1,0:T(8,128)S(1)}, f32[128,256]{1,0:T(8,128)}, u32[]{:S(2)}) %copy-start.2) | copy-done | bytes 131096
  6.4 0.0 copy-start.3
  6.4 0.8 %copy-done.3 = f32[2,8,8,128]{3,2,1,0:T(8,128)S(1)} copy-done((f32[2,8,8,128]{3,2,1,0:T(8,128)S(1)}, f32[2,8,8,128]{3,2,1,0:T(8,128)}, u32[]{:S(2)}) %copy-start.3) | copy-done | bytes 65560
  7.2 0.0 copy-start.4
  7.2 0.7 %copy-done.4 = s32[1,4]{1,0:T(1,128)S(1)} copy-done((s32[1,4]{1,0:T(1,128)S(1)}, s32[1,4]{1,0:T(1,128)}, u32[]{:S(2)}) %copy-start.4) | copy-done | bytes 40
  7.9 0.0 copy-start.5
  7.9 0.7 %copy-done.5 = s32[1,4,1]{1,2,0:T(1,128)S(1)} copy-done((s32[1,4,1]{1,2,0:T(1,128)S(1)}, s32[1,4,1]{1,2,0:T(1,128)}, u32[]{:S(2)}) %copy-start.5) | copy-done | bytes 40
  8.5 34.5 %shard_map.136 = (f32[3,8,16,128]{3,2,1,0:T(8,128)S(1)}, f32[8,128]{1,0:T(8,128)S(1)}, f32[54,64]{1,0:T(8,128)S(1)}, f32[1728,64]{1,0:T(8,128)}, f32[256,2048]{1,0:T(8,128)}, /*index=5*/f32[2,2048]{1,0:T(2,128)S(1)}) custom-call(s32[1,4]{1,0:T(1,128)S(1)} %copy-done.4, s32[1,4]{1,0:T(1,128)S(1)} %bitcast.27, f32[3,8,16,128]{3,2,1,0:T(8,128)S(1)} %copy-done.1, ...), custom_call_target="tpu_custom_call" | custom-call | tf_op jit(solution)/shard_map/pallas_call | solution.py:476
  43.0 0.0 copy-start.6
  43.0 0.6 %copy.22 = f32[2,1,4]{2,1,0:T(1,128)} copy(f32[2,1,4]{0,2,1:T(4,128)S(1)} %slice_bitcast_fusion) | data formatting | bytes 64
  43.7 0.6 %copy.23 = f32[1,54,64]{2,0,1:T(1,128)} copy(f32[1,54,64]{2,1,0:T(8,128)S(1)} %bitcast.25) | data formatting | bytes 27648
  44.3 0.7 %copy.30 = f32[3,8,16,128]{3,2,1,0:T(8,128)} copy(f32[3,8,16,128]{3,2,1,0:T(8,128)S(1)} %get-tuple-element.36) | data formatting | bytes 393216
  45.0 2.2 %copy.31 = f32[1,27,64,64]{3,2,1,0:T(8,128)} copy(f32[1,27,64,64]{3,2,1,0:T(8,128)} %bitcast.31) | data formatting | bytes 884736
  47.2 0.0 copy-done.6
  47.2 1.3 %copy.32 = f32[1,256,2048]{2,1,0:T(8,128)} copy(f32[1,256,2048]{2,1,0:T(8,128)S(1)} %bitcast.29) | data formatting | bytes 4194304
  48.5 0.6 %copy.33 = f32[1,2048,2]{1,2,0:T(2,128)} copy(f32[1,2048,2]{1,2,0:T(2,128)S(1)} %bitcast.26) | data formatting | bytes 32768
  (1 shorter events, 0.0 us)
Async XLA Ops:
  3.5 1.0 %copy-start = (bf16[1,27,64,64]{3,2,1,0:T(8,128)(2,1)S(1)}, bf16[1,27,64,64]{3,2,1,0:T(8,128)(2,1)}, u32[]{:S(2)}) copy-start(bf16[1,27,64,64]{3,2,1,0:T(8,128)(2,1)} %param.13) | copy-start | bytes 663556
  4.6 0.9 %copy-start.1 = (f32[3,8,16,128]{3,2,1,0:T(8,128)S(1)}, f32[3,8,16,128]{3,2,1,0:T(8,128)}, u32[]{:S(2)}) copy-start(f32[3,8,16,128]{3,2,1,0:T(8,128)} %field.1) | copy-start | bytes 589828
  5.5 0.9 %copy-start.2 = (f32[128,256]{1,0:T(8,128)S(1)}, f32[128,256]{1,0:T(8,128)}, u32[]{:S(2)}) copy-start(f32[128,256]{1,0:T(8,128)} %constant.8.clone.tab_z) | copy-start | bytes 393220
  6.4 0.8 %copy-start.3 = (f32[2,8,8,128]{3,2,1,0:T(8,128)S(1)}, f32[2,8,8,128]{3,2,1,0:T(8,128)}, u32[]{:S(2)}) copy-start(f32[2,8,8,128]{3,2,1,0:T(8,128)} %constant.7.clone.tab_x) | copy-start | bytes 196612
  7.2 0.7 %copy-start.4 = (s32[1,4]{1,0:T(1,128)S(1)}, s32[1,4]{1,0:T(1,128)}, u32[]{:S(2)}) copy-start(s32[1,4]{1,0:T(1,128)} %blocks.1) | copy-start | bytes 52
  7.9 0.7 %copy-start.5 = (s32[1,4,1]{1,2,0:T(1,128)S(1)}, s32[1,4,1]{1,2,0:T(1,128)}, u32[]{:S(2)}) copy-start(s32[1,4,1]{1,2,0:T(1,128)} %param.11) | copy-start | bytes 52
  43.0 4.2 %copy-start.6 = (f32[256,2048]{1,0:T(8,128)S(1)}, f32[256,2048]{1,0:T(8,128)}, u32[]{:S(2)}) copy-start(f32[256,2048]{1,0:T(8,128)} %get-tuple-element.16) | copy-start | bytes 6291460

commit v4 on v3

--- a/solution.py
+++ b/solution.py
@@ -117,12 +117,13 @@
 
 
 def network(
-    n, walls, per, blocks, members, field, tab_x, tab_z, k_first, k_second, k_back, w_hbm, w_out,
+    n, walls, per, blocks, members, w_out, k_first, field_hbm, k_second_hbm, tab_x_hbm, tab_z_hbm, w_hbm,
     new_field, stress, new_first, new_second, new_hidden, new_out,
     patch_out, tail_out, w_vmem, cols, pre_one, hid_pad, del_pad, mid_pad, pre_two, pooled,
     feat_in, tail_in, feat_all, delta_all, grads, grads_in, update, pred_in,
     patch_in, tail_wall, rows_all, tails_all, face_y, face_x, edge_x,
-    w_sem, sems, wall_sems, face_sems,
+    field, k_second, tab_x, tab_z, k_wide,
+    load_sems, sems, wall_sems, face_sems,
 ):
     me, wall = lax.axis_index("stream"), lax.axis_index("wall")
     barrier = pltpu.get_barrier_semaphore()
@@ -140,8 +141,15 @@
     points = 128 * batch
     share = 2048 // n
     samples = blocks.shape[1]
-    fetch = pltpu.make_async_copy(w_hbm, w_vmem, w_sem)
-    fetch.start()
+    loads = [
+        pltpu.make_async_copy(source, target, load_sems.at[i])
+        for i, (source, target) in enumerate((
+            (field_hbm, field), (k_second_hbm, k_second),
+            (tab_x_hbm, tab_x), (tab_z_hbm, tab_z), (w_hbm, w_vmem),
+        ))
+    ]
+    for load in loads:
+        load.start()
     slope, upper, lift = element_tables()
     scale_one = 1.0 / math.sqrt(54.0)
     scale_two = 1.0 / math.sqrt(1728.0)
@@ -179,6 +187,7 @@
         lax.broadcasted_iota(jnp.int32, (128, 128), 0) % 8
         == lax.broadcasted_iota(jnp.int32, (128, 128), 1) % 8, 1.0, 0.0
     ).astype(jnp.bfloat16)
+    loads[0].wait()
     for c in range(2):
         near = matmul(row_hot, field[2 * c].reshape(128, 128).astype(jnp.bfloat16))
         near = jnp.where(lane_w // 8 == (found & 15), near, 0.0).astype(jnp.bfloat16)
@@ -265,7 +274,10 @@
     columns = jnp.concatenate(
         [cols[pl.ds(slot, 64, stride=batch), :] for slot in range(batch)], axis=1
     ).astype(jnp.bfloat16)
-    first = matmul(columns, k_first[...], ((0,), (0,))) * scale_one
+    k_wide[...] = jnp.zeros((64, 64), jnp.float32)
+    k_wide[0:54, :] = k_first[...].astype(jnp.float32)
+    first = matmul(columns, k_wide[...].astype(jnp.bfloat16), ((0,), (0,))) * scale_one
+    loads[1].wait()
     for slot in range(batch):
         pre_one[pl.ds(slot, 128, stride=batch), :] = first[slot * 128 : slot * 128 + 128]
     value = pre_one[...]
@@ -299,7 +311,7 @@
         copies.append(remote(tail_in.at[0], tail_in.at[hop], sems, 2, hop, "stream", peer))
     for copy in copies:
         copy.start()
-    fetch.wait()
+    loads[4].wait()
 
     def dense(values):
         return jnp.concatenate(
@@ -339,9 +351,10 @@
         else:
             grads[start:896, 0:64] = grad_two[: 896 - start]
             grads[0 : start - 704, 64:128] = grad_two[896 - start :]
-        total = total + matmul(
-            window(del_pad, first_off, second_off), k_back[pair], ((1,), (1,))
-        )
+        k_back = jnp.concatenate(
+            [k_second[pair * 192 + c * 64 : pair * 192 + c * 64 + 64, :] for c in range(3)], axis=1
+        )
+        total = total + matmul(window(del_pad, first_off, second_off), k_back, ((1,), (1,)))
     pre_one[...] = total * scale_two * silu_slope(pre_one[...])
     delta_one = jnp.concatenate(
         [pre_one[pl.ds(slot, 128, stride=batch), :] for slot in range(batch)], axis=0
@@ -359,6 +372,8 @@
 
     for copy in faces_x:
         copy.wait_recv()
+    loads[2].wait()
+    loads[3].wait()
     flow = field[...]
     split = flow.reshape(3, 8, 2, 8, 128)
     grad_x = jnp.zeros((3, 8, 2, 8, 128), jnp.float32)
@@ -471,7 +486,6 @@
     tab_z = np.concatenate([axis_matrix(16, slope, lift).T, np.kron(np.eye(16), upper).T], axis=1)
     smem = pl.BlockSpec(memory_space=pltpu.SMEM)
     per = -(-896 // (n * 16)) * 16
-    k_back = k_second.reshape(9, 3, 64, 64).transpose(0, 2, 1, 3).reshape(9, 64, 192)
     vmem = pl.BlockSpec(memory_space=pltpu.VMEM)
     return pl.pallas_call(
         functools.partial(network, n, walls, per),
@@ -483,7 +497,7 @@
             jax.ShapeDtypeStruct((2048 // n, 2048), jnp.float32),
             jax.ShapeDtypeStruct((2, 2048), jnp.float32),
         ),
-        in_specs=[smem] * 2 + [vmem] * 6 + [pl.BlockSpec(memory_space=pl.ANY), vmem],
+        in_specs=[smem] * 2 + [vmem] * 2 + [pl.BlockSpec(memory_space=pltpu.HBM)] * 5,
         out_specs=(vmem,) * 6,
         scratch_shapes=[
             pltpu.VMEM((walls, 8, 256), jnp.float32),
@@ -511,18 +525,22 @@
             pltpu.VMEM((2, 3, 16, 128), jnp.float32),
             pltpu.VMEM((2, 3, 8, 128), jnp.float32),
             pltpu.VMEM((2, 3, 8, 128), jnp.float32),
-            pltpu.SemaphoreType.DMA,
+            pltpu.VMEM(field.shape, jnp.float32),
+            pltpu.VMEM((1728, 64), jnp.bfloat16),
+            pltpu.VMEM((2, 8, 8, 128), jnp.float32),
+            pltpu.VMEM((128, 256), jnp.float32),
+            pltpu.VMEM((64, 64), jnp.float32),
+            pltpu.SemaphoreType.DMA((5,)),
             pltpu.SemaphoreType.DMA((8, n)),
             pltpu.SemaphoreType.DMA((6, walls)),
             pltpu.SemaphoreType.DMA((4, 2)),
         ],
         compiler_params=pltpu.CompilerParams(
-            vmem_limit_bytes=52 * 1024 * 1024, collective_id=0, has_side_effects=True
+            vmem_limit_bytes=60 * 1024 * 1024, collective_id=0, has_side_effects=True
         ),
     )(
-        blocks, members, field, jnp.asarray(tab_x, jnp.float32), jnp.asarray(tab_z, jnp.float32),
-        jnp.pad(k_first, ((0, 10), (0, 0))), k_second.reshape(1728, 64), k_back, w_hidden,
-        w_out.T.astype(jnp.float32),
+        blocks, members, w_out.T.astype(jnp.float32), k_first, field, k_second.reshape(1728, 64),
+        jnp.asarray(tab_x, jnp.float32), jnp.asarray(tab_z, jnp.float32), w_hidden,
     )
 
 

time: 49.6 us -> 45.8 us (0.923)
  local copies, waits for them, and re-layouts: 13.3 us -> 8.58 us
  other arithmetic: 0.7 us -> 1.31 us
    unnamed x20 -> x10, local copies, waits for them, and re-layouts: 11 us -> 7.75 us
    another operation x1 -> x0, local copies, waits for them, and re-layouts: 1.25 us -> none  [train(): k_second.reshape(9, 3, 64, 64).transpose(0, 2, 1, 3).reshape(9, 64, 192)]
    broadcast_in_dim x1, local copies, waits for them, and re-layouts: 0.01 us -> 0.82 us  [body(): stress[:samples, :2].T[:, None, :]]
    pad x1 -> x0, local copies, waits for them, and re-layouts: 0.72 us -> none  [train(): jnp.pad(k_first, ((0, 10), (0, 0)))]
    convert_element_type x1, other arithmetic: 0.7 us -> 1.31 us  [train(): w_out.T.astype(jnp.float32)]
where the time goes in v4:
time: 45.8 us; the launch traced here: 45.4 us
  Pallas kernels  34.9 us (76%)
  local copies, waits for them, and re-layouts  8.58 us (19%)
  other arithmetic  1.31 us (3%)
  between operations  0.65 us (1%)
    pallas_call x1, Pallas kernels, train(): pl.pallas_call(functools.partial(network, n, walls, per), out_shape=(jax....  34.9 us
    unnamed x10, local copies, waits for them, and re-layouts  7.75 us
    convert_element_type x1, other arithmetic, train(): w_out.T.astype(jnp.float32)  1.31 us

profile of v4, /device:TPU:0, one launch (start us, length us, event | category | flops | bytes accessed | tf_op | source)
XLA Modules:
  0.0 45.4 jit_solution(275497319384719817)
XLA Ops:
  0.6 1.3 %convert_bitcast_fusion.w_out = f32[2,2048]{1,0:T(2,128)} fusion(bf16[1,2048,2]{1,2,0:T(2,128)(2,1)} %param.15), kind=kLoop, calls=%fused_computation | loop fusion | flops 4096 | bytes 24576 | tf_op jit(solution)/shard_map/convert_element_type | solution.py:542
  1.9 34.9 %shard_map.136 = (f32[3,8,16,128]{3,2,1,0:T(8,128)}, f32[8,128]{1,0:T(8,128)}, f32[54,64]{1,0:T(8,128)}, f32[1728,64]{1,0:T(8,128)}, f32[256,2048]{1,0:T(8,128)}, /*index=5*/f32[2,2048]{1,0:T(2,128)}) custom-call(s32[1,4]{1,0:T(1,128)} %blocks.1, s32[1,4]{1,0:T(1,128)} %bitcast.26, f32[2,2048]{1,0:T(2,128)} %convert_bitcast_fusion.w_out, ...), custom_call_target="tpu_custom_call" | custom-call | tf_op jit(solution)/shard_map/pallas_call | solution.py:490
  36.8 0.0 copy-start
  36.8 0.8 %slice_bitcast_fusion = f32[2,1,4]{0,2,1:T(4,128)S(1)} fusion(f32[8,128]{1,0:T(8,128)} %get-tuple-element.13), kind=kLoop, calls=%fused_computation.1 | loop fusion | bytes 64 | tf_op jit(solution)/shard_map/broadcast_in_dim | solution.py:553
  37.7 0.7 %copy.16 = f32[2,1,4]{2,1,0:T(1,128)} copy(f32[2,1,4]{0,2,1:T(4,128)S(1)} %slice_bitcast_fusion) | data formatting | bytes 64
  38.3 1.4 %copy.17 = f32[1,54,64]{2,0,1:T(1,128)} copy(f32[1,54,64]{2,1,0:T(8,128)} %bitcast.23) | data formatting | bytes 27648
  39.7 1.6 %copy.24 = f32[3,8,16,128]{3,2,1,0:T(8,128)} copy(f32[3,8,16,128]{3,2,1,0:T(8,128)} %get-tuple-element.30) | data formatting | bytes 393216
  41.3 2.2 %copy.25 = f32[1,27,64,64]{3,2,1,0:T(8,128)} copy(f32[1,27,64,64]{3,2,1,0:T(8,128)} %bitcast.21) | data formatting | bytes 884736
  43.5 0.0 copy-done
  43.5 0.0 copy-start.1
  43.5 1.3 %copy.26 = f32[1,256,2048]{2,1,0:T(8,128)} copy(f32[1,256,2048]{2,1,0:T(8,128)S(1)} %bitcast.20) | data formatting | bytes 4194304
  44.8 0.0 copy-done.1
  44.8 0.6 %copy.27 = f32[1,2048,2]{1,2,0:T(2,128)} copy(f32[1,2048,2]{1,2,0:T(2,128)S(1)} %bitcast.24) | data formatting | bytes 32768
Async XLA Ops:
  36.8 6.7 %copy-start = (f32[256,2048]{1,0:T(8,128)S(1)}, f32[256,2048]{1,0:T(8,128)}, u32[]{:S(2)}) copy-start(f32[256,2048]{1,0:T(8,128)} %get-tuple-element.16) | copy-start | bytes 6291460
  43.5 1.3 %copy-start.1 = (f32[2,2048]{1,0:T(2,128)S(1)}, f32[2,2048]{1,0:T(2,128)}, u32[]{:S(2)}) copy-start(f32[2,2048]{1,0:T(2,128)} %get-tuple-element.17) | copy-start | bytes 49156
